TPU v7x, 128 devices: a whole 4x4x4 slice. The times are simulated.
128 devices in a mesh: sweep: 4 (over y), row: 4 (over z), col: 8 (over x, core).
Axes of the slice: x: 4, y: 4, z: 4, core: 2. Of those that a mesh axis runs over, the one named last changes fastest.
Arguments:
- forcing: float32 [8, 2, 8, 32, 4096], P('sweep', None, None, 'row', 'col'), may hold values from -6 to 6
- inverses: bfloat16 [8, 2, 4096, 4096], P('sweep', None, 'col', 'row'), may hold values from -0.0625 to 0.0625
- stiffness: float32 [8, 4096], P('sweep'), may hold values from 0.5 to 2
- pml_layers: int32 [2], replicated, may hold values from 13 to 32
Outputs:
- solution: float32 [8, 2, 8, 32, 4096], P('sweep', None, None, 'row', 'col')
- residual: float32 [4, 2, 8, 32, 4096], P('sweep', None, None, 'row', 'col')
Inputs may be any that keep to these rules, and one draw needn't show every extreme that they name: pml_layers[0] counts damping planes at the top, pml_layers[1] at the bottom.
All inputs are finite; a program needn't handle non-finite values.
Results may differ from a plain program's by a relative error of at most 0.018.
Values may be sent and summed in bfloat16 or wider, within the bound.
A program may use at most 64 MiB of HBM per device.

v0:
```python
import jax
import jax.numpy as jnp
from jax import lax
from jax.sharding import PartitionSpec as P

GY = 64
PANEL_PLANES = 8


sigma_peak = 2.0


def shifted(block, axis, distance):
    devices = range(lax.axis_size(axis))
    route = [(i - distance, i) for i in devices if i - distance in devices]
    return lax.ppermute(block, axis, route)


def extended(block, sides, width):
    for axis, dim in sides:
        count = lax.axis_size(axis)
        forward = [(i, i + 1) for i in range(count - 1)]
        backward = [(target, source) for source, target in forward]
        low = lax.ppermute(
            lax.slice_in_dim(block, block.shape[dim] - width, None, axis=dim), axis, forward
        )
        high = lax.ppermute(lax.slice_in_dim(block, 0, width, axis=dim), axis, backward)
        block = jnp.concatenate([low, block, high], axis=dim)
    return block


def damping(layers, panel_index, panels_total):
    top_layers = layers[0].astype(jnp.float32)
    bottom_layers = layers[1].astype(jnp.float32)
    centre_plane = jnp.asarray(panel_index).astype(jnp.float32) * PANEL_PLANES + PANEL_PLANES / 2.0
    from_end = panels_total * PANEL_PLANES - centre_plane
    upper = jnp.maximum(top_layers - centre_plane, 0.0) / top_layers
    lower = jnp.maximum(bottom_layers - from_end, 0.0) / bottom_layers
    return sigma_peak * (upper * upper + lower * lower)


def complex_product(load_half, weights):
    real_part = jnp.einsum(
        "crk,kn->crn", load_half[0], weights[0], preferred_element_type=jnp.float32
    ) - jnp.einsum("crk,kn->crn", load_half[1], weights[1], preferred_element_type=jnp.float32)
    imag_part = jnp.einsum(
        "crk,kn->crn", load_half[0], weights[1], preferred_element_type=jnp.float32
    ) + jnp.einsum("crk,kn->crn", load_half[1], weights[0], preferred_element_type=jnp.float32)
    return jnp.stack([real_part, imag_part])


def plane_operator(wave_field, padded, stiff, sigma):
    length = wave_field.shape[-1]
    column = lax.broadcasted_iota(jnp.int32, (length,), 0) % GY
    lower_line = padded[..., 0:length]
    upper_line = padded[..., 2 * GY : 2 * GY + length]
    left_cell = jnp.where(column > 0, padded[..., GY - 1 : GY - 1 + length], 0.0)
    right_cell = jnp.where(column < GY - 1, padded[..., GY + 1 : GY + 1 + length], 0.0)
    beside = lower_line + upper_line + left_cell + right_cell
    centre = 6.0 - stiff
    absorb = stiff * sigma
    real_part = centre * wave_field[0] + absorb * wave_field[1] - beside[0]
    imag_part = centre * wave_field[1] - absorb * wave_field[0] - beside[1]
    return jnp.stack([real_part, imag_part])


def solve_panel(load_block, weights):
    partial_value = complex_product(lax.all_gather(load_block, "row", axis=2, tiled=True), weights)
    return lax.psum_scatter(partial_value, "col", scatter_dimension=1, tiled=True)


def redistribute(stacked):
    return lax.all_to_all(
        lax.all_to_all(stacked, "row", split_axis=3, concat_axis=4, tiled=True),
        "col",
        split_axis=4,
        concat_axis=2,
        tiled=True,
    )


def shards(forcing, inverses, stiffness, pml_layers):
    groups = lax.axis_size("sweep")
    group_index = lax.axis_index("sweep")
    local_rows = forcing.shape[3]
    front_cols = forcing.shape[4]
    pieces = 1
    block_rows = local_rows // pieces
    turns = groups + pieces - 1
    stiff_cols = lax.dynamic_slice_in_dim(
        stiffness[0], lax.axis_index("col") * front_cols, front_cols
    )
    sigma = damping(pml_layers, 2 * group_index, 2 * groups)
    previous = jnp.zeros((2, forcing.shape[2], block_rows, front_cols), jnp.float32)
    solved = jnp.zeros(forcing.shape, jnp.float32)
    even_loads = jnp.zeros(forcing.shape[1:], jnp.float32)
    applied = jnp.zeros((1,), jnp.float32)

    def one_turn(moment, state_tuple):
        previous, solved, even_loads, applied = state_tuple
        incoming = shifted(previous.astype(jnp.bfloat16), "sweep", 1).astype(previous.dtype)
        offset = moment - group_index
        active = (offset >= 0) & (offset < pieces)
        source_even = forcing[0]
        source_odd = forcing[1]
        load_even = source_even + incoming
        even_split = solve_panel(load_even.astype(jnp.bfloat16), inverses[0])
        even_block = redistribute(even_split[None])[0]
        load_odd = source_odd + even_block
        odd_split = solve_panel(load_odd.astype(jnp.bfloat16), inverses[1])
        odd_block = redistribute(odd_split[None])[0]

        def place(buffer, update):
            return jnp.where(active, update, buffer)

        solved = place(solved, jnp.stack([even_block, odd_block]))
        even_loads = place(even_loads, load_even)
        return (odd_block, solved, even_loads, applied)

    previous, solved, even_loads, applied = lax.fori_loop(
        0, turns, one_turn, (previous, solved, even_loads, applied)
    )
    wave_field = solved[0]
    padded = extended(wave_field.astype(jnp.bfloat16), (("col", 3),), GY).astype(wave_field.dtype)
    applied_even = plane_operator(wave_field, padded, stiff_cols, sigma)
    residual = even_loads - applied_even + solved[1]
    return (solved, residual[None])


def solution(mesh):
    return jax.shard_map(
        shards,
        mesh=mesh,
        in_specs=(
            P("sweep", None, None, "row", "col"),
            P("sweep", None, "col", "row"),
            P("sweep", None),
            P(),
        ),
        out_specs=(P("sweep", None, None, "row", "col"), P("sweep", None, None, "row", "col")),
        check_vma=False,
    )
```

profile of v0, /device:TPU:25, one launch (start us, length us, event | category | flops | bytes accessed | tf_op | source)
XLA Modules:
  0.0 1279.7 jit_solution(10214705557571595051)
XLA Ops:
  7.2 1256.0 %while.18 = (s32[]{:T(128)}, f32[2,8,8,512]{3,2,1,0:T(8,128)S(1)}, f32[2,2,8,8,512]{4,3,2,1,0:T(8,128)S(1)}, f32[2,8,8,512]{3,2,1,0:T(8,128)S(1)}, f32[2,2,8,8,5...) while((s32[]{:T(128)}, f32[2,8,8,512]{3,2,1,0:T(8,128)S(1)}, ...), condition=%wide.region_3.4_spmd.clone, body=%wide.region_0.3_spmd.clone.sunk | while | flops 2151546880 | bytes 108530208 | solution.py:120
  32.3 67.9 %all-reduce.9.cloned.1.call-done = f32[2,8,32,1024]{3,2,1,0:T(8,128)} async-done(((f32[2,8,32,1024]{3,2,1,0:T(8,128)}), f32[2,8,32,1024]{3,2,1,0:T(8,128)}) %all-reduce.9.cloned.1.call-update) | async-done | bytes 2097168 | tf_op jit(solution)/shard_map/while
  116.3 16.5 %reduce.8 = f32[4096,2,8]{2,1,0:T(2,128)} reduce(f32[4096,1,2,1,8]{4,3,2,1,0:T(1,128)} %bitcast.210, f32[]{:T(128)} %broadcast.78), dimensions={1,3}, to_apply=%bitcast.128.reduce_sub_computation | reduce | bytes 524292 | tf_op jit(solution)/shard_map/while
  141.0 13.1 %all_to_all.145 = f32[8,1,8192]{2,1,0:T(1,128)S(1)} all-to-all(f32[8,1,8192]{2,1,0:T(1,128)S(1)} %reshape.100), channel_id=1, replica_groups=mesh['sweep'=4,'row'=4,'col'=8] {'col'}, dimensions={0} | all-to-all | bytes 524288 | tf_op jit(solution)/shard_map/while/body/eval_jaxpr/all_to_all | solution.py:73
  186.8 65.3 %all-reduce.11.cloned.1.call-done = f32[2,8,32,1024]{3,2,1,0:T(8,128)} async-done(((f32[2,8,32,1024]{3,2,1,0:T(8,128)}), f32[2,8,32,1024]{3,2,1,0:T(8,128)}) %all-reduce.11.cloned.1.call-update) | async-done | bytes 2097168 | tf_op jit(solution)/shard_map/while
  268.2 16.4 %reduce.10 = f32[4096,2,8]{2,1,0:T(2,128)} reduce(f32[4096,1,2,1,8]{4,3,2,1,0:T(1,128)} %bitcast.211, f32[]{:T(128)} %broadcast.80), dimensions={1,3}, to_apply=%bitcast.130.reduce_sub_computation | reduce | bytes 524292 | tf_op jit(solution)/shard_map/while
  331.1 11.4 all_gather.18
  348.9 64.2 %all-reduce.9.cloned.1.call-done = f32[2,8,32,1024]{3,2,1,0:T(8,128)} async-done(((f32[2,8,32,1024]{3,2,1,0:T(8,128)}), f32[2,8,32,1024]{3,2,1,0:T(8,128)}) %all-reduce.9.cloned.1.call-update) | async-done | bytes 2097168 | tf_op jit(solution)/shard_map/while
  429.3 16.5 %reduce.8 = f32[4096,2,8]{2,1,0:T(2,128)} reduce(f32[4096,1,2,1,8]{4,3,2,1,0:T(1,128)} %bitcast.210, f32[]{:T(128)} %broadcast.78), dimensions={1,3}, to_apply=%bitcast.128.reduce_sub_computation | reduce | bytes 524292 | tf_op jit(solution)/shard_map/while
  454.0 13.1 %all_to_all.145 = f32[8,1,8192]{2,1,0:T(1,128)S(1)} all-to-all(f32[8,1,8192]{2,1,0:T(1,128)S(1)} %reshape.100), channel_id=1, replica_groups=mesh['sweep'=4,'row'=4,'col'=8] {'col'}, dimensions={0} | all-to-all | bytes 524288 | tf_op jit(solution)/shard_map/while/body/eval_jaxpr/all_to_all | solution.py:73
  499.8 65.3 %all-reduce.11.cloned.1.call-done = f32[2,8,32,1024]{3,2,1,0:T(8,128)} async-done(((f32[2,8,32,1024]{3,2,1,0:T(8,128)}), f32[2,8,32,1024]{3,2,1,0:T(8,128)}) %all-reduce.11.cloned.1.call-update) | async-done | bytes 2097168 | tf_op jit(solution)/shard_map/while
  581.2 16.4 %reduce.10 = f32[4096,2,8]{2,1,0:T(2,128)} reduce(f32[4096,1,2,1,8]{4,3,2,1,0:T(1,128)} %bitcast.211, f32[]{:T(128)} %broadcast.80), dimensions={1,3}, to_apply=%bitcast.130.reduce_sub_computation | reduce | bytes 524292 | tf_op jit(solution)/shard_map/while
  644.1 11.4 all_gather.18
  661.9 64.2 %all-reduce.9.cloned.1.call-done = f32[2,8,32,1024]{3,2,1,0:T(8,128)} async-done(((f32[2,8,32,1024]{3,2,1,0:T(8,128)}), f32[2,8,32,1024]{3,2,1,0:T(8,128)}) %all-reduce.9.cloned.1.call-update) | async-done | bytes 2097168 | tf_op jit(solution)/shard_map/while
  742.2 16.5 %reduce.8 = f32[4096,2,8]{2,1,0:T(2,128)} reduce(f32[4096,1,2,1,8]{4,3,2,1,0:T(1,128)} %bitcast.210, f32[]{:T(128)} %broadcast.78), dimensions={1,3}, to_apply=%bitcast.128.reduce_sub_computation | reduce | bytes 524292 | tf_op jit(solution)/shard_map/while
  767.0 13.1 %all_to_all.145 = f32[8,1,8192]{2,1,0:T(1,128)S(1)} all-to-all(f32[8,1,8192]{2,1,0:T(1,128)S(1)} %reshape.100), channel_id=1, replica_groups=mesh['sweep'=4,'row'=4,'col'=8] {'col'}, dimensions={0} | all-to-all | bytes 524288 | tf_op jit(solution)/shard_map/while/body/eval_jaxpr/all_to_all | solution.py:73
  812.8 65.3 %all-reduce.11.cloned.1.call-done = f32[2,8,32,1024]{3,2,1,0:T(8,128)} async-done(((f32[2,8,32,1024]{3,2,1,0:T(8,128)}), f32[2,8,32,1024]{3,2,1,0:T(8,128)}) %all-reduce.11.cloned.1.call-update) | async-done | bytes 2097168 | tf_op jit(solution)/shard_map/while
  894.2 16.4 %reduce.10 = f32[4096,2,8]{2,1,0:T(2,128)} reduce(f32[4096,1,2,1,8]{4,3,2,1,0:T(1,128)} %bitcast.211, f32[]{:T(128)} %broadcast.80), dimensions={1,3}, to_apply=%bitcast.130.reduce_sub_computation | reduce | bytes 524292 | tf_op jit(solution)/shard_map/while
  957.0 11.4 all_gather.18
  974.9 64.2 %all-reduce.9.cloned.1.call-done = f32[2,8,32,1024]{3,2,1,0:T(8,128)} async-done(((f32[2,8,32,1024]{3,2,1,0:T(8,128)}), f32[2,8,32,1024]{3,2,1,0:T(8,128)}) %all-reduce.9.cloned.1.call-update) | async-done | bytes 2097168 | tf_op jit(solution)/shard_map/while
  1055.2 16.5 %reduce.8 = f32[4096,2,8]{2,1,0:T(2,128)} reduce(f32[4096,1,2,1,8]{4,3,2,1,0:T(1,128)} %bitcast.210, f32[]{:T(128)} %broadcast.78), dimensions={1,3}, to_apply=%bitcast.128.reduce_sub_computation | reduce | bytes 524292 | tf_op jit(solution)/shard_map/while
  1080.0 13.1 %all_to_all.145 = f32[8,1,8192]{2,1,0:T(1,128)S(1)} all-to-all(f32[8,1,8192]{2,1,0:T(1,128)S(1)} %reshape.100), channel_id=1, replica_groups=mesh['sweep'=4,'row'=4,'col'=8] {'col'}, dimensions={0} | all-to-all | bytes 524288 | tf_op jit(solution)/shard_map/while/body/eval_jaxpr/all_to_all | solution.py:73
  1125.8 65.4 %all-reduce.11.cloned.1.call-done = f32[2,8,32,1024]{3,2,1,0:T(8,128)} async-done(((f32[2,8,32,1024]{3,2,1,0:T(8,128)}), f32[2,8,32,1024]{3,2,1,0:T(8,128)}) %all-reduce.11.cloned.1.call-update) | async-done | bytes 2097168 | tf_op jit(solution)/shard_map/while
  1207.3 16.4 %reduce.10 = f32[4096,2,8]{2,1,0:T(2,128)} reduce(f32[4096,1,2,1,8]{4,3,2,1,0:T(1,128)} %bitcast.211, f32[]{:T(128)} %broadcast.80), dimensions={1,3}, to_apply=%bitcast.130.reduce_sub_computation | reduce | bytes 524292 | tf_op jit(solution)/shard_map/while
  (231 shorter events, 523.1 us)
Async XLA Ops:
  7.2 1261.2 %copy-start.4 = (s32[2]{0:T(128)S(1)}, s32[2]{0:T(128)}, u32[]{:S(2)}) copy-start(s32[2]{0:T(128)} %param.9) | copy-start | bytes 28
  7.2 1263.2 %slice-start = ((f32[2,4096]{1,0:T(2,128)}), f32[1,4096]{1,0:T(1,128)S(1)}, s32[]{:S(2)}) async-start(f32[2,4096]{1,0:T(2,128)} %param.8), calls=%async_computation.6 | async-start | bytes 32768 | tf_op jit(solution)/shard_map/slice | solution.py:91
  7.3 92.9 %all-reduce.9.cloned.1.call-start = ((), (), s32[]{:S(2)}) async-start(), calls=%async_computation.4 | async-start | bytes 4194304 | tf_op jit(solution)/shard_map/while
  7.3 6.3 collective-permute-start
  8.6 20.5 %copy-start = (bf16[2,2,512,1024]{3,2,1,0:T(8,128)(2,1)S(1)}, bf16[2,2,512,1024]{3,2,1,0:T(8,128)(2,1)}, u32[]{:S(2)}) copy-start(bf16[2,2,512,1024]{3,2,1,0:T(8,128)(2,1)} %get-tuple-element.261) | copy-start | bytes 12582916 | tf_op jit(solution)/shard_map/while
  31.6 220.6 %all-reduce.11.cloned.1.call-start = ((), (), s32[]{:S(2)}) async-start(), calls=%async_computation.5 | async-start | bytes 4194304 | tf_op jit(solution)/shard_map/while
  293.6 13.9 %all-to-all-start.3 = ((f32[8,1,8192]{2,1,0:T(1,128)}), f32[8,1,8192]{2,1,0:T(1,128)S(1)}, u32[]{:S(2)}, u32[]{:S(2)}) async-start(f32[8,1,8192]{2,1,0:T(1,128)} %reshape.102), calls=%async_computation.3 | async-start | bytes 524288 | tf_op jit(solution)/shard_map/while/body/eval_jaxpr/all_to_all | solution.py:73
  324.2 88.9 %all-reduce.9.cloned.1.call-start = ((), (), s32[]{:S(2)}) async-start(), calls=%async_computation.4 | async-start | bytes 4194304 | tf_op jit(solution)/shard_map/while
  324.3 5.7 collective-permute-start
  325.6 20.2 %copy-start = (bf16[2,2,512,1024]{3,2,1,0:T(8,128)(2,1)S(1)}, bf16[2,2,512,1024]{3,2,1,0:T(8,128)(2,1)}, u32[]{:S(2)}) copy-start(bf16[2,2,512,1024]{3,2,1,0:T(8,128)(2,1)} %get-tuple-element.261) | copy-start | bytes 12582916 | tf_op jit(solution)/shard_map/while
  348.3 216.9 %all-reduce.11.cloned.1.call-start = ((), (), s32[]{:S(2)}) async-start(), calls=%async_computation.5 | async-start | bytes 4194304 | tf_op jit(solution)/shard_map/while
  606.6 13.9 %all-to-all-start.3 = ((f32[8,1,8192]{2,1,0:T(1,128)}), f32[8,1,8192]{2,1,0:T(1,128)S(1)}, u32[]{:S(2)}, u32[]{:S(2)}) async-start(f32[8,1,8192]{2,1,0:T(1,128)} %reshape.102), calls=%async_computation.3 | async-start | bytes 524288 | tf_op jit(solution)/shard_map/while/body/eval_jaxpr/all_to_all | solution.py:73
  637.2 88.9 %all-reduce.9.cloned.1.call-start = ((), (), s32[]{:S(2)}) async-start(), calls=%async_computation.4 | async-start | bytes 4194304 | tf_op jit(solution)/shard_map/while
  637.3 5.7 collective-permute-start
  638.6 20.2 %copy-start = (bf16[2,2,512,1024]{3,2,1,0:T(8,128)(2,1)S(1)}, bf16[2,2,512,1024]{3,2,1,0:T(8,128)(2,1)}, u32[]{:S(2)}) copy-start(bf16[2,2,512,1024]{3,2,1,0:T(8,128)(2,1)} %get-tuple-element.261) | copy-start | bytes 12582916 | tf_op jit(solution)/shard_map/while
  661.2 216.9 %all-reduce.11.cloned.1.call-start = ((), (), s32[]{:S(2)}) async-start(), calls=%async_computation.5 | async-start | bytes 4194304 | tf_op jit(solution)/shard_map/while
  919.6 13.9 %all-to-all-start.3 = ((f32[8,1,8192]{2,1,0:T(1,128)}), f32[8,1,8192]{2,1,0:T(1,128)S(1)}, u32[]{:S(2)}, u32[]{:S(2)}) async-start(f32[8,1,8192]{2,1,0:T(1,128)} %reshape.102), calls=%async_computation.3 | async-start | bytes 524288 | tf_op jit(solution)/shard_map/while/body/eval_jaxpr/all_to_all | solution.py:73
  950.2 88.9 %all-reduce.9.cloned.1.call-start = ((), (), s32[]{:S(2)}) async-start(), calls=%async_computation.4 | async-start | bytes 4194304 | tf_op jit(solution)/shard_map/while
  950.2 5.7 collective-permute-start
  951.6 20.2 %copy-start = (bf16[2,2,512,1024]{3,2,1,0:T(8,128)(2,1)S(1)}, bf16[2,2,512,1024]{3,2,1,0:T(8,128)(2,1)}, u32[]{:S(2)}) copy-start(bf16[2,2,512,1024]{3,2,1,0:T(8,128)(2,1)} %get-tuple-element.261) | copy-start | bytes 12582916 | tf_op jit(solution)/shard_map/while
  974.2 217.0 %all-reduce.11.cloned.1.call-start = ((), (), s32[]{:S(2)}) async-start(), calls=%async_computation.5 | async-start | bytes 4194304 | tf_op jit(solution)/shard_map/while
  1232.6 13.9 %all-to-all-start.3 = ((f32[8,1,8192]{2,1,0:T(1,128)}), f32[8,1,8192]{2,1,0:T(1,128)S(1)}, u32[]{:S(2)}, u32[]{:S(2)}) async-start(f32[8,1,8192]{2,1,0:T(1,128)} %reshape.102), calls=%async_computation.3 | async-start | bytes 524288 | tf_op jit(solution)/shard_map/while/body/eval_jaxpr/all_to_all | solution.py:73
  1263.4 7.1 collective-permute-start.1
  1266.5 5.2 collective-permute-start.2
  (13 other events, 131.4 us)
Sparse Core Ops, SparseCore 0:
  31.7 68.3 all-reduce.8
  187.0 65.1 all-reduce.10
  348.4 64.6 all-reduce.8
  499.9 65.1 all-reduce.10
  661.4 64.6 all-reduce.8
  812.9 65.1 all-reduce.10
  974.4 64.6 all-reduce.8
  1125.9 65.2 all-reduce.10
where the time goes:
time: 1280 us
  waiting for transfers between devices  567 us (44%)
  local copies, waits for them, and re-layouts  247 us (19%)
  blocking collectives  214 us (17%)
  other arithmetic  161 us (13%)
  starting transfers between devices  39.9 us (3%)
  matrix products  33.6 us (3%)
  between operations  15.6 us (1%)
    while x16, waiting for transfers between devices  522 us
    while x60, local copies, waits for them, and re-layouts  153 us
    while x8, other arithmetic  132 us
    all_gather x8, blocking collectives, solve_panel(): lax.all_gather(load_block, 'row', axis=2, tiled=True)  85.9 us
    all_to_all x8, blocking collectives, redistribute(): lax.all_to_all(stacked, 'row', split_axis=3, concat_axis=4, tiled=True)  75.8 us
    all_to_all x4, blocking collectives, redistribute(): lax.all_to_all(lax.all_to_all(stacked, 'row', split_axis=3, concat_axis=4...  52.5 us
    all_to_all x16, local copies, waits for them, and re-layouts, redistribute(): lax.all_to_all(lax.all_to_all(stacked, 'row', split_axis=3, concat_axis=4...  45.3 us
    all_to_all x8, local copies, waits for them, and re-layouts, redistribute(): lax.all_to_all(stacked, 'row', split_axis=3, concat_axis=4, tiled=True)  34.1 us
  transfers between devices with their start and end apart: 18, of which 17 were waited for; matrix products, arithmetic and copies ran while one was open for 0% of the time, Pallas kernels for 0%

commit v1 on v0

v1 whole, which is shorter than its diff:
```python
import functools

import jax
import jax.numpy as jnp
from jax import lax
from jax.experimental import pallas as pl
from jax.experimental.pallas import tpu as pltpu
from jax.sharding import PartitionSpec as P

GY = 64
PANEL_PLANES = 8
SIGMA_PEAK = 2.0
MESH = pl.DeviceIdType.MESH
F32 = jnp.float32
BF16 = jnp.bfloat16
ROWS = 16


def sweep_kernel(
    groups, nrow, ncol,
    forcing, inverses, stiffness, pml, solved, residual,
    weights, loads, parts, sib, total, arrive, onward, next_forcing, edge_out, edge_in,
    w_sem, load_recv, load_send, sib_recv, sib_send, arr_recv, arr_send, fwd_send,
    nf_sem, edge_send, edge_recv,
):
    chunks = forcing.shape[2]
    width = forcing.shape[4]
    chips = ncol // 2
    g, r, c = lax.axis_index("sweep"), lax.axis_index("row"), lax.axis_index("col")
    chip, core = c // 2, lax.rem(c, 2)
    sibling = 2 * chip + 1 - core
    home_chip = r == chip
    first, last = g == 0, g == groups - 1
    left_end, right_end = c == 0, c == ncol - 1

    def column(other_row):
        return (g, other_row, c)

    def target(other_row):
        return (g, other_row, 2 * r + core)

    w_copies = [
        pltpu.make_async_copy(inverses.at[p], weights.at[p], w_sem.at[p]) for p in range(2)
    ]
    for copy in w_copies:
        copy.start()

    barrier = pltpu.get_barrier_semaphore()

    def greet(device):
        pl.semaphore_signal(barrier, inc=1, device_id=device, device_id_type=MESH)

    for step in range(1, nrow):
        greet(column(lax.rem(r + step, nrow)))
    greet((g, r, sibling))
    for other in range(nrow):
        @pl.when(jnp.logical_not(jnp.logical_and(home_chip, other == r)))
        def _():
            greet(target(other))
    for other in range(chips):
        @pl.when(jnp.logical_not(jnp.logical_and(home_chip, other == chip)))
        def _():
            greet((g, chip, 2 * other + core))
    for other in range(nrow):
        @pl.when(jnp.logical_not(last))
        def _():
            greet((g + 1, other, c))

        @pl.when(jnp.logical_not(first))
        def _():
            greet((g - 1, other, c))

    @pl.when(jnp.logical_not(left_end))
    def _():
        greet((g, r, c - 1))

    @pl.when(jnp.logical_not(right_end))
    def _():
        greet((g, r, c + 1))

    @pl.when(first)
    def _():
        for k in range(chunks):
            loads[0, k, r] = forcing[0, :, k].reshape(ROWS, width).astype(BF16)

    @pl.when(left_end)
    def _():
        edge_in[0] = jnp.zeros_like(edge_in[0])

    @pl.when(right_end)
    def _():
        edge_in[1] = jnp.zeros_like(edge_in[1])

    expected = (nrow - 1) + 1 + nrow + chips
    expected = expected - 2 * home_chip.astype(jnp.int32)
    expected = expected + nrow * (2 - first.astype(jnp.int32) - last.astype(jnp.int32))
    expected = expected + 2 - left_end.astype(jnp.int32) - right_end.astype(jnp.int32)
    pl.semaphore_wait(barrier, expected)

    def load_copy(p, k, step):
        return pltpu.make_async_remote_copy(
            src_ref=loads.at[p, k, r], dst_ref=loads.at[p, k, r],
            send_sem=load_send.at[p, k, step - 1], recv_sem=load_recv.at[p, k],
            device_id=column(lax.rem(r + step, nrow)), device_id_type=MESH,
        )

    def forward_copy(k, other):
        return pltpu.make_async_remote_copy(
            src_ref=onward.at[k], dst_ref=loads.at[0, k, r],
            send_sem=fwd_send.at[k, other], recv_sem=load_recv.at[0, k],
            device_id=(g + 1, other, c), device_id_type=MESH,
        )

    def sib_copy(p, k):
        return pltpu.make_async_remote_copy(
            src_ref=parts.at[p, k, 1 - core], dst_ref=sib.at[p, k],
            send_sem=sib_send.at[p, k], recv_sem=sib_recv.at[p, k],
            device_id=(g, r, sibling), device_id_type=MESH,
        )

    def home_copy(p, k, other):
        return pltpu.make_async_remote_copy(
            src_ref=total.at[p, k, other], dst_ref=arrive.at[p, k, chip],
            send_sem=arr_send.at[p, k, other], recv_sem=arr_recv.at[p, k],
            device_id=target(other), device_id_type=MESH,
        )

    def nf_copy():
        return pltpu.make_async_remote_copy(
            src_ref=forcing.at[0], dst_ref=next_forcing,
            send_sem=nf_sem.at[0], recv_sem=nf_sem.at[1],
            device_id=(g - 1, r, c), device_id_type=MESH,
        )

    def edge_copy(side):
        return pltpu.make_async_remote_copy(
            src_ref=edge_out.at[side], dst_ref=edge_in.at[1 - side],
            send_sem=edge_send.at[side], recv_sem=edge_recv.at[1 - side],
            device_id=(g, r, c - 1 + 2 * side), device_id_type=MESH,
        )

    def landed(buffer, count, sem):
        some = buffer.at[pl.ds(0, count)]
        pltpu.make_async_copy(some, some, sem).wait()

    def wait_loads(p, k):
        if p == 1:
            landed(loads.at[p, k], nrow - 1, load_recv.at[p, k])
        else:
            @pl.when(first)
            def _():
                landed(loads.at[p, k], nrow - 1, load_recv.at[p, k])

            @pl.when(jnp.logical_not(first))
            def _():
                landed(loads.at[p, k], nrow, load_recv.at[p, k])

    def multiply(p, k):
        wait_loads(p, k)
        rows = nrow * ROWS
        left = loads[p, k].reshape(rows, width)
        by_real = jnp.dot(left, weights[p, 0], preferred_element_type=F32)
        by_imag = jnp.dot(left, weights[p, 1], preferred_element_type=F32)
        by_real = by_real.reshape(nrow, 2, 8, 2 * width)
        by_imag = by_imag.reshape(nrow, 2, 8, 2 * width)
        real = by_real[:, 0] - by_imag[:, 1]
        imag = by_real[:, 1] + by_imag[:, 0]
        both = jnp.concatenate([real[:, None], imag[:, None]], axis=1).reshape(nrow, ROWS, 2 * width)
        both = both.astype(BF16)
        parts[p, k, 0] = both[:, :, :width]
        parts[p, k, 1] = both[:, :, width:]
        sib_copy(p, k).start()

    def combine(p, k):
        sib_copy(p, k).wait_recv()
        whole = parts[p, k, core].astype(F32) + sib[p, k].astype(F32)
        total[p, k] = whole.astype(BF16)

        @pl.when(home_chip)
        def _():
            arrive[p, k, chip] = total[p, k, r]

        for other in range(nrow):
            @pl.when(jnp.logical_not(jnp.logical_and(home_chip, other == r)))
            def _():
                home_copy(p, k, other).start()

    def gather_sum(p, k):
        @pl.when(home_chip)
        def _():
            landed(arrive.at[p, k], chips - 1, arr_recv.at[p, k])

        @pl.when(jnp.logical_not(home_chip))
        def _():
            landed(arrive.at[p, k], chips, arr_recv.at[p, k])

        value = jnp.sum(arrive[p, k].astype(F32), axis=0)
        solved[p, 0, k] = value[:8]
        solved[p, 1, k] = value[8:]
        return value

    def finish_even(k):
        value = gather_sum(0, k)
        source = forcing[1, :, k].reshape(ROWS, width)
        loads[1, k, r] = (value + source).astype(BF16)
        for step in range(1, nrow):
            load_copy(1, k, step).start()
        edge_out[0, k] = value[:, :128].astype(BF16)
        edge_out[1, k] = value[:, width - 128 :].astype(BF16)

    def finish_odd(k):
        value = gather_sum(1, k)

        @pl.when(jnp.logical_not(last))
        def _():
            source = next_forcing[:, k].reshape(ROWS, width)
            onward[k] = (value + source).astype(BF16)
            for other in range(nrow):
                forward_copy(k, other).start()

    @pl.when(first)
    def _():
        for k in range(chunks):
            for step in range(1, nrow):
                load_copy(0, k, step).start()

    @pl.when(jnp.logical_not(first))
    def _():
        nf_copy().start()

    for copy in w_copies:
        copy.wait()

    @pl.when(jnp.logical_not(last))
    def _():
        nf_copy().wait_recv()

    def at(turn, lag, task):
        k = turn - lag

        @pl.when(jnp.logical_and(k >= 0, k < chunks))
        def _():
            task(k)

    def one_turn(turn, carry):
        at(turn, 0, lambda k: multiply(0, k))
        at(turn, 4, finish_odd)
        at(turn, 0, lambda k: combine(0, k))
        at(turn, 2, lambda k: multiply(1, k))
        at(turn, 1, finish_even)

        @pl.when(turn == chunks)
        def _():
            @pl.when(jnp.logical_not(left_end))
            def _():
                edge_copy(0).start()

            @pl.when(jnp.logical_not(right_end))
            def _():
                edge_copy(1).start()

        at(turn, 2, lambda k: combine(1, k))
        return carry

    lax.fori_loop(0, chunks + 4, one_turn, 0)

    @pl.when(jnp.logical_not(left_end))
    def _():
        edge_copy(0).wait_send()

    @pl.when(jnp.logical_not(right_end))
    def _():
        edge_copy(1).wait_send()

    @pl.when(jnp.logical_not(left_end))
    def _():
        edge_copy(1).wait_recv()

    @pl.when(jnp.logical_not(right_end))
    def _():
        edge_copy(0).wait_recv()

    def spread(number):
        return jnp.full((8, width), number, jnp.int32).astype(F32)

    top, bottom = spread(pml[0]), spread(pml[1])
    centre_plane = spread(2 * g).astype(F32) * PANEL_PLANES + PANEL_PLANES / 2.0
    from_end = 2 * groups * PANEL_PLANES - centre_plane
    upper = jnp.maximum(top - centre_plane, 0.0) / top
    lower = jnp.maximum(bottom - from_end, 0.0) / bottom
    sigma = SIGMA_PEAK * (upper * upper + lower * lower)
    begin = pl.multiple_of(c * width, 128)
    stiff = jnp.broadcast_to(stiffness[0:1, pl.ds(begin, width)], (8, width))
    centre = 6.0 - stiff
    absorb = stiff * sigma
    line = lax.rem(lax.broadcasted_iota(jnp.int32, (ROWS, width), 1), GY)
    not_low, not_high = line > 0, line < GY - 1

    def one_residual(k, carry):
        real, imag = solved[0, 0, k], solved[0, 1, k]
        wave = jnp.concatenate([real, imag], axis=0)
        padded = jnp.concatenate(
            [edge_in[0, k].astype(F32), wave, edge_in[1, k].astype(F32)], axis=1
        )
        span = width + 256

        def moved(distance):
            turned = pltpu.roll(padded, distance % span, 1)
            return turned[:, 128 : 128 + width]

        beside = moved(GY) + moved(-GY)
        beside = beside + jnp.where(not_low, moved(1), 0.0) + jnp.where(not_high, moved(-1), 0.0)
        load = loads[0, k, r].astype(F32)
        real_applied = centre * real + absorb * imag - beside[:8]
        imag_applied = centre * imag - absorb * real - beside[8:]
        residual[0, 0, k] = load[:8] - real_applied + solved[1, 0, k]
        residual[0, 1, k] = load[8:] - imag_applied + solved[1, 1, k]
        return carry

    lax.fori_loop(0, chunks, one_residual, 0)

    def drain(k, carry):
        for p in range(2):
            sib_copy(p, k).wait_send()
            for other in range(nrow):
                @pl.when(jnp.logical_not(jnp.logical_and(home_chip, other == r)))
                def _():
                    home_copy(p, k, other).wait_send()
        for step in range(1, nrow):
            load_copy(1, k, step).wait_send()

        @pl.when(first)
        def _():
            for step in range(1, nrow):
                load_copy(0, k, step).wait_send()

        @pl.when(jnp.logical_not(last))
        def _():
            for other in range(nrow):
                forward_copy(k, other).wait_send()

        return carry

    lax.fori_loop(0, chunks, drain, 0)

    @pl.when(jnp.logical_not(first))
    def _():
        nf_copy().wait_send()


def shards(forcing, inverses, stiffness, pml_layers):
    groups, nrow, ncol = (lax.axis_size(name) for name in ("sweep", "row", "col"))
    _, _, chunks, shot_rows, width = forcing.shape
    chips = ncol // 2
    dma = pltpu.SemaphoreType.DMA
    vmem = pl.BlockSpec(memory_space=pltpu.VMEM)
    return pl.pallas_call(
        functools.partial(sweep_kernel, groups, nrow, ncol),
        name="sweep",
        out_shape=(
            jax.ShapeDtypeStruct(forcing.shape, F32),
            jax.ShapeDtypeStruct((1,) + forcing.shape[1:], F32),
        ),
        in_specs=[
            vmem,
            pl.BlockSpec(memory_space=pl.ANY),
            vmem,
            pl.BlockSpec(memory_space=pltpu.SMEM),
        ],
        out_specs=(vmem, vmem),
        scratch_shapes=[
            pltpu.VMEM(inverses.shape, BF16),
            pltpu.VMEM((2, chunks, nrow, ROWS, width), BF16),
            pltpu.VMEM((2, chunks, 2, nrow, ROWS, width), BF16),
            pltpu.VMEM((2, chunks, nrow, ROWS, width), BF16),
            pltpu.VMEM((2, chunks, nrow, ROWS, width), BF16),
            pltpu.VMEM((2, chunks, chips, ROWS, width), BF16),
            pltpu.VMEM((chunks, ROWS, width), BF16),
            pltpu.VMEM(forcing.shape[1:], F32),
            pltpu.VMEM((2, chunks, ROWS, 128), BF16),
            pltpu.VMEM((2, chunks, ROWS, 128), BF16),
            dma((2,)),
            dma((2, chunks)),
            dma((2, chunks, nrow - 1)),
            dma((2, chunks)),
            dma((2, chunks)),
            dma((2, chunks)),
            dma((2, chunks, nrow)),
            dma((chunks, nrow)),
            dma((2,)),
            dma((2,)),
            dma((2,)),
        ],
        compiler_params=pltpu.CompilerParams(
            collective_id=0, has_side_effects=True, vmem_limit_bytes=40 * 1024 * 1024
        ),
        cost_estimate=pl.CostEstimate(
            flops=2 * 2 * 8 * 256 * 512 * 1024, bytes_accessed=6 * 2**20, transcendentals=0
        ),
    )(forcing, inverses, stiffness, pml_layers)


def solution(mesh):
    return jax.shard_map(
        shards,
        mesh=mesh,
        in_specs=(
            P("sweep", None, None, "row", "col"),
            P("sweep", None, "col", "row"),
            P("sweep", None),
            P(),
        ),
        out_specs=(P("sweep", None, None, "row", "col"), P("sweep", None, None, "row", "col")),
        check_vma=False,
    )
```

time: 1280 us -> 180 us (0.14)
  waiting for transfers between devices: 567 us -> 0 us
  local copies, waits for them, and re-layouts: 247 us -> 6.13 us
  blocking collectives: 214 us -> 0 us
  Pallas kernels: 0 us -> 173 us
  other arithmetic: 161 us -> 0 us
  starting transfers between devices: 39.9 us -> 0 us
  matrix products: 33.6 us -> 0 us
  between operations: 15.6 us -> 0.65 us
    while x16 -> x0, waiting for transfers between devices: 522 us -> none
    pallas_call x0 -> x1, Pallas kernels: none -> 173 us  [shards(): pl.pallas_call(functools.partial(sweep_kernel, groups, nrow, ncol), name=...]
    while x60 -> x0, local copies, waits for them, and re-layouts: 153 us -> none
    while x8 -> x0, other arithmetic: 132 us -> none
    all_to_all x12 -> x0, blocking collectives: 128 us -> none  [the longest x8 75.8 us: redistribute(): lax.all_to_all(stacked, 'row', split_axis=3, concat_axis=4, tiled=True)]
    all_gather x8 -> x0, blocking collectives: 85.9 us -> none  [solve_panel(): lax.all_gather(load_block, 'row', axis=2, tiled=True)]
    all_to_all x24 -> x0, local copies, waits for them, and re-layouts: 79.4 us -> none  [the longest x16 45.3 us: redistribute(): lax.all_to_all(lax.all_to_all(stacked, 'row', split_axis=3, concat_axis=4...]
    dot_general x32 -> x0, matrix products: 33.6 us -> none  [the longest x8 13.3 us: complex_product(): jnp.einsum('crk,kn->crn', load_half[0], weights[1], preferred_element_typ...]
  transfers between devices with their start and end apart: 18 -> 0, of which waited for: 17 -> 0; matrix products, arithmetic and copies ran while one was open for 0% -> 0% of each run, Pallas kernels for 0% -> 0%
where the time goes in v1:
time: 180 us; the launch traced here: 179 us
  Pallas kernels  173 us (96%)
  local copies, waits for them, and re-layouts  6.13 us (3%)
    pallas_call x1, Pallas kernels, shards(): pl.pallas_call(functools.partial(sweep_kernel, groups, nrow, ncol), name=...  173 us
    unnamed x10, local copies, waits for them, and re-layouts  6.13 us

profile of v1, /device:TPU:25, one launch (start us, length us, event | category | flops | bytes accessed | tf_op | source)
XLA Modules:
  0.0 179.4 jit_solution(18337618033456332635)
XLA Ops:
  0.6 0.0 copy-start
  0.6 2.2 %copy-done = bf16[2,2,512,1024]{3,2,1,0:T(8,128)(2,1)S(1)} copy-done((bf16[2,2,512,1024]{3,2,1,0:T(8,128)(2,1)S(1)}, bf16[2,2,512,1024]{3,2,1,0:T(8,128)(2,1)}, u32[]{:S(2)}) %copy-start) | copy-done | bytes 4194328
  2.8 0.0 copy-start.1
  2.8 1.0 copy-done.1
  3.9 0.0 copy-start.2
  3.9 0.8 copy-done.2
  4.6 0.0 copy-start.3
  4.6 0.7 copy-done.3
  5.3 172.7 %sweep.1 = (f32[2,2,8,8,512]{4,3,2,1,0:T(8,128)S(1)}, f32[1,2,8,8,512]{4,3,2,1,0:T(8,128)S(1)}) custom-call(f32[2,2,8,8,512]{4,3,2,1,0:T(8,128)S(1)} %copy-done.1, bf16[2,2,512,1024]{3,2,1,0:T(8,128)(2,1)S(1)} %copy-done, f32[2,4096]{1,0:T(2,128)S(1)} %copy-done.2, s32[2]{0:T(128)S(1)} %copy-done.3), custom_call_target="tpu_custom_call" | custom-call | flops 4294967296 | bytes 6291456 | tf_op jit(solution)/shard_map/sweep/pallas_call | solution.py:357
  177.9 0.8 copy.8
  178.7 0.7 copy.9
Async XLA Ops:
  0.6 2.2 %copy-start = (bf16[2,2,512,1024]{3,2,1,0:T(8,128)(2,1)S(1)}, bf16[2,2,512,1024]{3,2,1,0:T(8,128)(2,1)}, u32[]{:S(2)}) copy-start(bf16[2,2,512,1024]{3,2,1,0:T(8,128)(2,1)} %inverses.1) | copy-start | bytes 12582916
  2.8 1.0 copy-start.1
  3.9 0.8 copy-start.2
  4.6 0.7 copy-start.3

commit v2 on v1

--- a/solution.py
+++ b/solution.py
@@ -13,36 +13,45 @@
 MESH = pl.DeviceIdType.MESH
 F32 = jnp.float32
 BF16 = jnp.bfloat16
+ORDER = (
+    ("Ae", 0), ("Co", 7), ("Ao", 4), ("Be", 0), ("Bo", 4), ("Re", 1), ("Ro", 5), ("Ce", 2),
+)
 ROWS = 16
 
 
 def sweep_kernel(
     groups, nrow, ncol,
-    forcing, inverses, stiffness, pml, solved, residual,
-    weights, loads, parts, sib, total, arrive, onward, next_forcing, edge_out, edge_in,
-    w_sem, load_recv, load_send, sib_recv, sib_send, arr_recv, arr_send, fwd_send,
+    forcing_hbm, inverses, stiffness, pml, solved, residual,
+    weights, sources, loads, parts, sib, total, middle, arrive, onward, next_forcing, edge_out, edge_in,
+    stiff_here, w_sem, in_sem, mid_send, mid_recv, load_recv, load_send, sib_recv, sib_send, arr_recv, arr_send, fwd_send,
     nf_sem, edge_send, edge_recv,
 ):
-    chunks = forcing.shape[2]
-    width = forcing.shape[4]
+    chunks = forcing_hbm.shape[2]
+    width = forcing_hbm.shape[4]
+    forcing = sources
     chips = ncol // 2
     g, r, c = lax.axis_index("sweep"), lax.axis_index("row"), lax.axis_index("col")
     chip, core = c // 2, lax.rem(c, 2)
     sibling = 2 * chip + 1 - core
-    home_chip = r == chip
     first, last = g == 0, g == groups - 1
     left_end, right_end = c == 0, c == ncol - 1
 
     def column(other_row):
         return (g, other_row, c)
 
-    def target(other_row):
-        return (g, other_row, 2 * r + core)
+    def along(other_chip):
+        return (g, r, 2 * other_chip + core)
 
     w_copies = [
         pltpu.make_async_copy(inverses.at[p], weights.at[p], w_sem.at[p]) for p in range(2)
     ]
-    for copy in w_copies:
+    begin = pl.multiple_of(c * width, 128)
+    in_copies = [
+        pltpu.make_async_copy(forcing_hbm.at[0], sources.at[0], in_sem.at[0]),
+        pltpu.make_async_copy(forcing_hbm.at[1], sources.at[1], in_sem.at[1]),
+        pltpu.make_async_copy(stiffness, stiff_here, in_sem.at[2]),
+    ]
+    for copy in in_copies + w_copies:
         copy.start()
 
     barrier = pltpu.get_barrier_semaphore()
@@ -53,14 +62,8 @@
     for step in range(1, nrow):
         greet(column(lax.rem(r + step, nrow)))
     greet((g, r, sibling))
-    for other in range(nrow):
-        @pl.when(jnp.logical_not(jnp.logical_and(home_chip, other == r)))
-        def _():
-            greet(target(other))
-    for other in range(chips):
-        @pl.when(jnp.logical_not(jnp.logical_and(home_chip, other == chip)))
-        def _():
-            greet((g, chip, 2 * other + core))
+    for step in range(1, chips):
+        greet(along(lax.rem(chip + step, chips)))
     for other in range(nrow):
         @pl.when(jnp.logical_not(last))
         def _():
@@ -78,6 +81,8 @@
     def _():
         greet((g, r, c + 1))
 
+    in_copies[0].wait()
+
     @pl.when(first)
     def _():
         for k in range(chunks):
@@ -91,8 +96,7 @@
     def _():
         edge_in[1] = jnp.zeros_like(edge_in[1])
 
-    expected = (nrow - 1) + 1 + nrow + chips
-    expected = expected - 2 * home_chip.astype(jnp.int32)
+    expected = (nrow - 1) + 1 + (chips - 1)
     expected = expected + nrow * (2 - first.astype(jnp.int32) - last.astype(jnp.int32))
     expected = expected + 2 - left_end.astype(jnp.int32) - right_end.astype(jnp.int32)
     pl.semaphore_wait(barrier, expected)
@@ -118,16 +122,25 @@
             device_id=(g, r, sibling), device_id_type=MESH,
         )
 
-    def home_copy(p, k, other):
-        return pltpu.make_async_remote_copy(
-            src_ref=total.at[p, k, other], dst_ref=arrive.at[p, k, chip],
-            send_sem=arr_send.at[p, k, other], recv_sem=arr_recv.at[p, k],
-            device_id=target(other), device_id_type=MESH,
+    def middle_copy(p, k, step):
+        other = lax.rem(r + step, nrow)
+        return pltpu.make_async_remote_copy(
+            src_ref=total.at[p, k, other], dst_ref=middle.at[p, k, r],
+            send_sem=mid_send.at[p, k, step - 1], recv_sem=mid_recv.at[p, k],
+            device_id=column(other), device_id_type=MESH,
+        )
+
+    def home_copy(p, k, step):
+        other = lax.rem(chip + step, chips)
+        return pltpu.make_async_remote_copy(
+            src_ref=middle.at[p, k, other], dst_ref=arrive.at[p, k, chip],
+            send_sem=arr_send.at[p, k, step - 1], recv_sem=arr_recv.at[p, k],
+            device_id=along(other), device_id_type=MESH,
         )
 
     def nf_copy():
         return pltpu.make_async_remote_copy(
-            src_ref=forcing.at[0], dst_ref=next_forcing,
+            src_ref=sources.at[0], dst_ref=next_forcing,
             send_sem=nf_sem.at[0], recv_sem=nf_sem.at[1],
             device_id=(g - 1, r, c), device_id_type=MESH,
         )
@@ -175,25 +188,18 @@
         sib_copy(p, k).wait_recv()
         whole = parts[p, k, core].astype(F32) + sib[p, k].astype(F32)
         total[p, k] = whole.astype(BF16)
-
-        @pl.when(home_chip)
-        def _():
-            arrive[p, k, chip] = total[p, k, r]
-
-        for other in range(nrow):
-            @pl.when(jnp.logical_not(jnp.logical_and(home_chip, other == r)))
-            def _():
-                home_copy(p, k, other).start()
+        middle[p, k, r] = total[p, k, r]
+        for step in range(1, nrow):
+            middle_copy(p, k, step).start()
+
+    def pass_on(p, k):
+        landed(middle.at[p, k], nrow - 1, mid_recv.at[p, k])
+        for step in range(1, chips):
+            home_copy(p, k, step).start()
+        arrive[p, k, chip] = middle[p, k, chip]
 
     def gather_sum(p, k):
-        @pl.when(home_chip)
-        def _():
-            landed(arrive.at[p, k], chips - 1, arr_recv.at[p, k])
-
-        @pl.when(jnp.logical_not(home_chip))
-        def _():
-            landed(arrive.at[p, k], chips, arr_recv.at[p, k])
-
+        landed(arrive.at[p, k], chips - 1, arr_recv.at[p, k])
         value = jnp.sum(arrive[p, k].astype(F32), axis=0)
         solved[p, 0, k] = value[:8]
         solved[p, 1, k] = value[8:]
@@ -228,7 +234,7 @@
     def _():
         nf_copy().start()
 
-    for copy in w_copies:
+    for copy in in_copies[1:] + w_copies:
         copy.wait()
 
     @pl.when(jnp.logical_not(last))
@@ -242,27 +248,34 @@
         def _():
             task(k)
 
+    steps = {
+        "Ae": lambda k: multiply(0, k),
+        "Be": lambda k: combine(0, k),
+        "Re": lambda k: pass_on(0, k),
+        "Ce": finish_even,
+        "Ao": lambda k: multiply(1, k),
+        "Bo": lambda k: combine(1, k),
+        "Ro": lambda k: pass_on(1, k),
+        "Co": finish_odd,
+    }
+
     def one_turn(turn, carry):
-        at(turn, 0, lambda k: multiply(0, k))
-        at(turn, 4, finish_odd)
-        at(turn, 0, lambda k: combine(0, k))
-        at(turn, 2, lambda k: multiply(1, k))
-        at(turn, 1, finish_even)
-
-        @pl.when(turn == chunks)
-        def _():
-            @pl.when(jnp.logical_not(left_end))
-            def _():
-                edge_copy(0).start()
-
-            @pl.when(jnp.logical_not(right_end))
-            def _():
-                edge_copy(1).start()
-
-        at(turn, 2, lambda k: combine(1, k))
+        for name, lag in ORDER:
+            at(turn, lag, steps[name])
+            if name == "Ce":
+                @pl.when(turn == chunks - 1 + lag)
+                def _():
+                    @pl.when(jnp.logical_not(left_end))
+                    def _():
+                        edge_copy(0).start()
+
+                    @pl.when(jnp.logical_not(right_end))
+                    def _():
+                        edge_copy(1).start()
+
         return carry
 
-    lax.fori_loop(0, chunks + 4, one_turn, 0)
+    lax.fori_loop(0, chunks + max(lag for _, lag in ORDER), one_turn, 0)
 
     @pl.when(jnp.logical_not(left_end))
     def _():
@@ -289,8 +302,7 @@
     upper = jnp.maximum(top - centre_plane, 0.0) / top
     lower = jnp.maximum(bottom - from_end, 0.0) / bottom
     sigma = SIGMA_PEAK * (upper * upper + lower * lower)
-    begin = pl.multiple_of(c * width, 128)
-    stiff = jnp.broadcast_to(stiffness[0:1, pl.ds(begin, width)], (8, width))
+    stiff = jnp.broadcast_to(stiff_here[0:1, pl.ds(begin, width)], (8, width))
     centre = 6.0 - stiff
     absorb = stiff * sigma
     line = lax.rem(lax.broadcasted_iota(jnp.int32, (ROWS, width), 1), GY)
@@ -322,10 +334,10 @@
     def drain(k, carry):
         for p in range(2):
             sib_copy(p, k).wait_send()
-            for other in range(nrow):
-                @pl.when(jnp.logical_not(jnp.logical_and(home_chip, other == r)))
-                def _():
-                    home_copy(p, k, other).wait_send()
+            for step in range(1, nrow):
+                middle_copy(p, k, step).wait_send()
+            for step in range(1, chips):
+                home_copy(p, k, step).wait_send()
         for step in range(1, nrow):
             load_copy(1, k, step).wait_send()
 
@@ -362,16 +374,18 @@
             jax.ShapeDtypeStruct((1,) + forcing.shape[1:], F32),
         ),
         in_specs=[
-            vmem,
             pl.BlockSpec(memory_space=pl.ANY),
-            vmem,
+            pl.BlockSpec(memory_space=pl.ANY),
+            pl.BlockSpec(memory_space=pl.ANY),
             pl.BlockSpec(memory_space=pltpu.SMEM),
         ],
         out_specs=(vmem, vmem),
         scratch_shapes=[
             pltpu.VMEM(inverses.shape, BF16),
+            pltpu.VMEM(forcing.shape, F32),
             pltpu.VMEM((2, chunks, nrow, ROWS, width), BF16),
             pltpu.VMEM((2, chunks, 2, nrow, ROWS, width), BF16),
+            pltpu.VMEM((2, chunks, nrow, ROWS, width), BF16),
             pltpu.VMEM((2, chunks, nrow, ROWS, width), BF16),
             pltpu.VMEM((2, chunks, nrow, ROWS, width), BF16),
             pltpu.VMEM((2, chunks, chips, ROWS, width), BF16),
@@ -379,20 +393,24 @@
             pltpu.VMEM(forcing.shape[1:], F32),
             pltpu.VMEM((2, chunks, ROWS, 128), BF16),
             pltpu.VMEM((2, chunks, ROWS, 128), BF16),
+            pltpu.VMEM(stiffness.shape, F32),
             dma((2,)),
+            dma((3,)),
+            dma((2, chunks, nrow - 1)),
+            dma((2, chunks)),
             dma((2, chunks)),
             dma((2, chunks, nrow - 1)),
             dma((2, chunks)),
             dma((2, chunks)),
             dma((2, chunks)),
-            dma((2, chunks, nrow)),
+            dma((2, chunks, chips - 1)),
             dma((chunks, nrow)),
             dma((2,)),
             dma((2,)),
             dma((2,)),
         ],
         compiler_params=pltpu.CompilerParams(
-            collective_id=0, has_side_effects=True, vmem_limit_bytes=40 * 1024 * 1024
+            collective_id=0, has_side_effects=True, vmem_limit_bytes=60 * 1024 * 1024
         ),
         cost_estimate=pl.CostEstimate(
             flops=2 * 2 * 8 * 256 * 512 * 1024, bytes_accessed=6 * 2**20, transcendentals=0

time: 180 us -> 140 us (0.78)
  Pallas kernels: 173 us -> 135 us
  local copies, waits for them, and re-layouts: 6.13 us -> 3.54 us
    pallas_call x1, Pallas kernels: 173 us -> 135 us  [shards(): pl.pallas_call(functools.partial(sweep_kernel, groups, nrow, ncol), name=...]
    unnamed x10 -> x2, local copies, waits for them, and re-layouts: 6.13 us -> 3.54 us
where the time goes in v2:
time: 140 us
  Pallas kernels  135 us (96%)
  local copies, waits for them, and re-layouts  3.54 us (3%)
    pallas_call x1, Pallas kernels, shards(): pl.pallas_call(functools.partial(sweep_kernel, groups, nrow, ncol), name=...  135 us
    unnamed x2, local copies, waits for them, and re-layouts  3.54 us

profile of v2, /device:TPU:25, one launch (start us, length us, event | category | flops | bytes accessed | tf_op | source)
XLA Modules:
  0.0 139.5 jit_solution(10212361363209071202)
XLA Ops:
  0.6 135.3 %sweep.1 = (f32[2,2,8,8,512]{4,3,2,1,0:T(8,128)}, f32[1,2,8,8,512]{4,3,2,1,0:T(8,128)}) custom-call(f32[2,2,8,8,512]{4,3,2,1,0:T(8,128)} %forcing_hbm.1, bf16[2,2,512,1024]{3,2,1,0:T(8,128)(2,1)} %inverses.1, f32[2,4096]{1,0:T(2,128)} %stiffness.1, s32[2]{0:T(128)} %pml.1), custom_call_target="tpu_custom_call" | custom-call | flops 4294967296 | bytes 6291456 | tf_op jit(solution)/shard_map/sweep/pallas_call | solution.py:369
  136.0 1.9 %copy.8 = f32[2,2,8,8,512]{4,3,2,1,0:T(8,128)} copy(f32[2,2,8,8,512]{4,3,2,1,0:T(8,128)} %get-tuple-element.4) | data formatting | bytes 1048576
  137.8 1.7 %copy.9 = f32[1,2,8,8,512]{4,3,2,1,0:T(8,128)} copy(f32[1,2,8,8,512]{4,3,2,1,0:T(8,128)} %get-tuple-element.5) | data formatting | bytes 524288

commit v3 on v2

--- a/solution.py
+++ b/solution.py
@@ -13,9 +13,14 @@
 MESH = pl.DeviceIdType.MESH
 F32 = jnp.float32
 BF16 = jnp.bfloat16
-ORDER = (
-    ("Ae", 0), ("Co", 7), ("Ao", 4), ("Be", 0), ("Bo", 4), ("Re", 1), ("Ro", 5), ("Ce", 2),
+PLAIN_ORDER = (
+    ("Ce", 3), ("Ae", 0), ("Co", 7), ("Ao", 4), ("Be", 0), ("Re", 1), ("Bo", 4), ("Ro", 5), ("Rs", 29), ("Dr", 36),
 )
+TURNED_ORDER = (
+    ("Ce", 4), ("Co", 5), ("Rs", 5), ("Ao", 3), ("Ae", 0), ("Dr", 5), ("Be", 0), ("Bo", 3), ("Ct", 1),
+)
+PLAIN_GROUPS = 2
+SUB = 1
 ROWS = 16
 
 
@@ -23,8 +28,10 @@
     groups, nrow, ncol,
     forcing_hbm, inverses, stiffness, pml, solved, residual,
     weights, sources, loads, parts, sib, total, middle, arrive, onward, next_forcing, edge_out, edge_in,
-    stiff_here, w_sem, in_sem, mid_send, mid_recv, load_recv, load_send, sib_recv, sib_send, arr_recv, arr_send, fwd_send,
-    nf_sem, edge_send, edge_recv,
+    stiff_here, turned_out, turned_forcing, held, home_out, home_in,
+    w_sem, in_sem, turn_sem, out_send, held_recv, pass_send, part_recv,
+    home_send, home_recv, mid_send, mid_recv,
+    load_recv, load_send, sib_recv, sib_send, arr_recv, arr_send, fwd_send, nf_sem, edge_send, edge_recv,
 ):
     chunks = forcing_hbm.shape[2]
     width = forcing_hbm.shape[4]
@@ -35,6 +42,11 @@
     sibling = 2 * chip + 1 - core
     first, last = g == 0, g == groups - 1
     left_end, right_end = c == 0, c == ncol - 1
+    plain = g < PLAIN_GROUPS
+    later = jnp.logical_not(plain)
+    diagonal = r == chip
+    partner = (g, chip, 2 * r + core)
+    crossed = jnp.logical_and(later, jnp.logical_not(diagonal))
 
     def column(other_row):
         return (g, other_row, c)
@@ -51,8 +63,12 @@
         pltpu.make_async_copy(forcing_hbm.at[1], sources.at[1], in_sem.at[1]),
         pltpu.make_async_copy(stiffness, stiff_here, in_sem.at[2]),
     ]
-    for copy in in_copies + w_copies:
+    for copy in in_copies + w_copies[:1]:
         copy.start()
+
+    @pl.when(jnp.logical_not(crossed))
+    def _():
+        w_copies[1].start()
 
     barrier = pltpu.get_barrier_semaphore()
 
@@ -73,6 +89,13 @@
         def _():
             greet((g - 1, other, c))
 
+    @pl.when(crossed)
+    def _():
+        for step in range(1, chips):
+            greet((g, chip, 2 * lax.rem(chip + step, chips) + core))
+        for step in range(1, nrow):
+            greet((g, lax.rem(r + step, nrow), 2 * r + core))
+
     @pl.when(jnp.logical_not(left_end))
     def _():
         greet((g, r, c - 1))
@@ -82,6 +105,16 @@
         greet((g, r, c + 1))
 
     in_copies[0].wait()
+    in_copies[1].wait()
+
+    @pl.when(later)
+    def _():
+        for k in range(chunks):
+            turned_out[k] = forcing[1, :, k].reshape(ROWS, width).astype(BF16)
+
+    @pl.when(jnp.logical_and(later, diagonal))
+    def _():
+        turned_forcing[...] = turned_out[...]
 
     @pl.when(first)
     def _():
@@ -98,20 +131,21 @@
 
     expected = (nrow - 1) + 1 + (chips - 1)
     expected = expected + nrow * (2 - first.astype(jnp.int32) - last.astype(jnp.int32))
+    expected = expected + (nrow + chips - 2) * crossed.astype(jnp.int32)
     expected = expected + 2 - left_end.astype(jnp.int32) - right_end.astype(jnp.int32)
     pl.semaphore_wait(barrier, expected)
 
     def load_copy(p, k, step):
         return pltpu.make_async_remote_copy(
             src_ref=loads.at[p, k, r], dst_ref=loads.at[p, k, r],
-            send_sem=load_send.at[p, k, step - 1], recv_sem=load_recv.at[p, k],
+            send_sem=load_send.at[p, k], recv_sem=load_recv.at[p, k],
             device_id=column(lax.rem(r + step, nrow)), device_id_type=MESH,
         )
 
     def forward_copy(k, other):
         return pltpu.make_async_remote_copy(
             src_ref=onward.at[k], dst_ref=loads.at[0, k, r],
-            send_sem=fwd_send.at[k, other], recv_sem=load_recv.at[0, k],
+            send_sem=fwd_send.at[k], recv_sem=load_recv.at[0, k],
             device_id=(g + 1, other, c), device_id_type=MESH,
         )
 
@@ -126,17 +160,103 @@
         other = lax.rem(r + step, nrow)
         return pltpu.make_async_remote_copy(
             src_ref=total.at[p, k, other], dst_ref=middle.at[p, k, r],
-            send_sem=mid_send.at[p, k, step - 1], recv_sem=mid_recv.at[p, k],
+            send_sem=mid_send.at[p, k], recv_sem=mid_recv.at[p, k],
             device_id=column(other), device_id_type=MESH,
+        )
+
+    def row_copy(p, k, step):
+        other = lax.rem(chip + step, chips)
+        return pltpu.make_async_remote_copy(
+            src_ref=total.at[p, k, other], dst_ref=arrive.at[p, k, chip],
+            send_sem=arr_send.at[p, k], recv_sem=arr_recv.at[p, k],
+            device_id=along(other), device_id_type=MESH,
         )
 
     def home_copy(p, k, step):
         other = lax.rem(chip + step, chips)
         return pltpu.make_async_remote_copy(
             src_ref=middle.at[p, k, other], dst_ref=arrive.at[p, k, chip],
-            send_sem=arr_send.at[p, k, step - 1], recv_sem=arr_recv.at[p, k],
+            send_sem=arr_send.at[p, k], recv_sem=arr_recv.at[p, k],
             device_id=along(other), device_id_type=MESH,
         )
+
+    def row_load_copy(k, step):
+        return pltpu.make_async_remote_copy(
+            src_ref=loads.at[1, k, chip], dst_ref=loads.at[1, k, chip],
+            send_sem=load_send.at[1, k], recv_sem=load_recv.at[1, k],
+            device_id=along(lax.rem(chip + step, chips)), device_id_type=MESH,
+        )
+
+    def solved_copy(k):
+        return pltpu.make_async_remote_copy(
+            src_ref=home_out.at[k], dst_ref=home_in.at[k],
+            send_sem=home_send.at[k], recv_sem=home_recv.at[k],
+            device_id=partner, device_id_type=MESH,
+        )
+
+    part_rows = width // nrow
+
+    def part(index):
+        start = index * part_rows
+        if not isinstance(index, int):
+            start = pl.multiple_of(start, part_rows)
+        return pl.ds(start, part_rows)
+
+    def turned_source():
+        return pltpu.make_async_remote_copy(
+            src_ref=turned_out, dst_ref=turned_forcing,
+            send_sem=turn_sem.at[1], recv_sem=turn_sem.at[2],
+            device_id=partner, device_id_type=MESH,
+        )
+
+    def out_copy(half, q, direct):
+        rows = part(q)
+        if direct:
+            landing, landed_sem = weights.at[1, half, rows], part_recv.at[half, q]
+        else:
+            landing, landed_sem = held.at[half, r], held_recv.at[half, r]
+        return pltpu.make_async_remote_copy(
+            src_ref=inverses.at[1, half, rows], dst_ref=landing,
+            send_sem=out_send.at[half, q], recv_sem=landed_sem,
+            device_id=(g, chip, 2 * q + core) if half == 0 or direct else (g, q, c),
+            device_id_type=MESH,
+        )
+
+    def held_part(half, source):
+        here = held.at[half, source]
+        return pltpu.make_async_copy(here, here, held_recv.at[half, source])
+
+    def pass_copy(half, source):
+        index = chip if half == 0 else r
+        return pltpu.make_async_remote_copy(
+            src_ref=held.at[half, source], dst_ref=weights.at[1, half, part(index)],
+            send_sem=pass_send.at[half, source], recv_sem=part_recv.at[half, index],
+            device_id=(g, r if half == 0 else chip, 2 * source + core), device_id_type=MESH,
+        )
+
+    def last_part(half, q):
+        here = weights.at[1, half, part(q)]
+        return pltpu.make_async_copy(here, here, part_recv.at[half, q])
+
+    def each_out(act):
+        for half, step in [(half, step) for half in range(2) for step in range(nrow)]:
+                q = lax.rem((chip if half == 0 else r) + step, nrow)
+
+                @pl.when(r == q)
+                def _():
+                    act(out_copy(half, q, True))
+
+                @pl.when(r != q)
+                def _():
+                    act(out_copy(half, q, False))
+
+    def each_pass(act):
+        for half, step in [(half, step) for half in range(2) for step in range(nrow)]:
+                source = lax.rem((r if half == 0 else r) + step, nrow)
+
+                @pl.when(jnp.logical_and(source != r, source != chip))
+                def _():
+                    act(half, source)
 
     def nf_copy():
         return pltpu.make_async_remote_copy(
@@ -145,12 +265,18 @@
             device_id=(g - 1, r, c), device_id_type=MESH,
         )
 
-    def edge_copy(side):
-        return pltpu.make_async_remote_copy(
-            src_ref=edge_out.at[side], dst_ref=edge_in.at[1 - side],
-            send_sem=edge_send.at[side], recv_sem=edge_recv.at[1 - side],
+    def edge_copy(side, k):
+        return pltpu.make_async_remote_copy(
+            src_ref=edge_out.at[side, k], dst_ref=edge_in.at[1 - side, k],
+            send_sem=edge_send.at[side, k], recv_sem=edge_recv.at[1 - side, k],
             device_id=(g, r, c - 1 + 2 * side), device_id_type=MESH,
         )
+
+    def each_edge(act):
+        for side, end in ((0, left_end), (1, right_end)):
+            @pl.when(jnp.logical_not(end))
+            def _():
+                act(side)
 
     def landed(buffer, count, sem):
         some = buffer.at[pl.ds(0, count)]
@@ -159,6 +285,12 @@
     def wait_loads(p, k):
         if p == 1:
             landed(loads.at[p, k], nrow - 1, load_recv.at[p, k])
+
+            @pl.when(jnp.logical_and(crossed, k == 0))
+            def _():
+                for half in range(2):
+                    for q in range(nrow):
+                        last_part(half, q).wait()
         else:
             @pl.when(first)
             def _():
@@ -187,35 +319,48 @@
     def combine(p, k):
         sib_copy(p, k).wait_recv()
         whole = parts[p, k, core].astype(F32) + sib[p, k].astype(F32)
+
         total[p, k] = whole.astype(BF16)
-        middle[p, k, r] = total[p, k, r]
-        for step in range(1, nrow):
-            middle_copy(p, k, step).start()
+
+        def to_rows():
+            middle[p, k, r] = total[p, k, r]
+            for step in range(1, nrow):
+                middle_copy(p, k, step).start()
+
+        if p == 1:
+            to_rows()
+        else:
+            pl.when(plain)(to_rows)
+
+            @pl.when(later)
+            def _():
+                arrive[p, k, chip] = total[p, k, chip]
+                for step in range(1, chips):
+                    row_copy(p, k, step).start()
+
+    def row_sum(p, k):
+        landed(arrive.at[p, k], chips - 1, arr_recv.at[p, k])
+        return jnp.sum(arrive[p, k].astype(F32), axis=0)
+
+    def middle_landed(p, k):
+        landed(middle.at[p, k], nrow - 1, mid_recv.at[p, k])
 
     def pass_on(p, k):
-        landed(middle.at[p, k], nrow - 1, mid_recv.at[p, k])
+        middle_landed(p, k)
         for step in range(1, chips):
             home_copy(p, k, step).start()
         arrive[p, k, chip] = middle[p, k, chip]
 
-    def gather_sum(p, k):
-        landed(arrive.at[p, k], chips - 1, arr_recv.at[p, k])
-        value = jnp.sum(arrive[p, k].astype(F32), axis=0)
+    def keep(p, k, value):
         solved[p, 0, k] = value[:8]
         solved[p, 1, k] = value[8:]
-        return value
-
-    def finish_even(k):
-        value = gather_sum(0, k)
-        source = forcing[1, :, k].reshape(ROWS, width)
-        loads[1, k, r] = (value + source).astype(BF16)
-        for step in range(1, nrow):
-            load_copy(1, k, step).start()
-        edge_out[0, k] = value[:, :128].astype(BF16)
-        edge_out[1, k] = value[:, width - 128 :].astype(BF16)
-
-    def finish_odd(k):
-        value = gather_sum(1, k)
+        if p == 0:
+            edge_out[0, k] = value[:, :128].astype(BF16)
+            edge_out[1, k] = value[:, width - 128 :].astype(BF16)
+            each_edge(lambda side: edge_copy(side, k).start())
+
+    def forward(k, value):
+        keep(1, k, value)
 
         @pl.when(jnp.logical_not(last))
         def _():
@@ -224,6 +369,46 @@
             for other in range(nrow):
                 forward_copy(k, other).start()
 
+    def turned_sum(k):
+        own = row_sum(0, k)
+        loads[1, k, chip] = (own + turned_forcing[k].astype(F32)).astype(BF16)
+        for step in range(1, chips):
+            row_load_copy(k, step).start()
+
+        @pl.when(diagonal)
+        def _():
+            keep(0, k, own)
+
+        @pl.when(crossed)
+        def _():
+            home_out[k] = own.astype(BF16)
+            solved_copy(k).start()
+
+    def finish_even(k):
+        @pl.when(plain)
+        def _():
+            value = row_sum(0, k)
+            keep(0, k, value)
+            source = forcing[1, :, k].reshape(ROWS, width)
+            loads[1, k, r] = (value + source).astype(BF16)
+            for step in range(1, nrow):
+                load_copy(1, k, step).start()
+
+        @pl.when(crossed)
+        def _():
+            solved_copy(k).wait_recv()
+            keep(0, k, home_in[k].astype(F32))
+
+    def finish_odd(k):
+        @pl.when(plain)
+        def _():
+            forward(k, row_sum(1, k))
+
+        @pl.when(later)
+        def _():
+            middle_landed(1, k)
+            forward(k, jnp.sum(middle[1, k].astype(F32), axis=0))
+
     @pl.when(first)
     def _():
         for k in range(chunks):
@@ -234,64 +419,33 @@
     def _():
         nf_copy().start()
 
-    for copy in in_copies[1:] + w_copies:
+    @pl.when(crossed)
+    def _():
+        turned_source().start()
+        each_out(lambda copy: copy.start())
+
+    for copy in in_copies[2:] + w_copies[:1]:
         copy.wait()
 
+    @pl.when(jnp.logical_not(crossed))
+    def _():
+        w_copies[1].wait()
+
+    @pl.when(later)
+    def _():
+        def pass_part(half, source):
+            held_part(half, source).wait()
+            pass_copy(half, source).start()
+
+        each_pass(pass_part)
+
+    @pl.when(crossed)
+    def _():
+        turned_source().wait_recv()
+
     @pl.when(jnp.logical_not(last))
     def _():
         nf_copy().wait_recv()
-
-    def at(turn, lag, task):
-        k = turn - lag
-
-        @pl.when(jnp.logical_and(k >= 0, k < chunks))
-        def _():
-            task(k)
-
-    steps = {
-        "Ae": lambda k: multiply(0, k),
-        "Be": lambda k: combine(0, k),
-        "Re": lambda k: pass_on(0, k),
-        "Ce": finish_even,
-        "Ao": lambda k: multiply(1, k),
-        "Bo": lambda k: combine(1, k),
-        "Ro": lambda k: pass_on(1, k),
-        "Co": finish_odd,
-    }
-
-    def one_turn(turn, carry):
-        for name, lag in ORDER:
-            at(turn, lag, steps[name])
-            if name == "Ce":
-                @pl.when(turn == chunks - 1 + lag)
-                def _():
-                    @pl.when(jnp.logical_not(left_end))
-                    def _():
-                        edge_copy(0).start()
-
-                    @pl.when(jnp.logical_not(right_end))
-                    def _():
-                        edge_copy(1).start()
-
-        return carry
-
-    lax.fori_loop(0, chunks + max(lag for _, lag in ORDER), one_turn, 0)
-
-    @pl.when(jnp.logical_not(left_end))
-    def _():
-        edge_copy(0).wait_send()
-
-    @pl.when(jnp.logical_not(right_end))
-    def _():
-        edge_copy(1).wait_send()
-
-    @pl.when(jnp.logical_not(left_end))
-    def _():
-        edge_copy(1).wait_recv()
-
-    @pl.when(jnp.logical_not(right_end))
-    def _():
-        edge_copy(0).wait_recv()
 
     def spread(number):
         return jnp.full((8, width), number, jnp.int32).astype(F32)
@@ -308,7 +462,8 @@
     line = lax.rem(lax.broadcasted_iota(jnp.int32, (ROWS, width), 1), GY)
     not_low, not_high = line > 0, line < GY - 1
 
-    def one_residual(k, carry):
+    def one_residual(k):
+        each_edge(lambda side: edge_copy(1 - side, k).wait_recv())
         real, imag = solved[0, 0, k], solved[0, 1, k]
         wave = jnp.concatenate([real, imag], axis=0)
         padded = jnp.concatenate(
@@ -327,33 +482,78 @@
         imag_applied = centre * imag - absorb * real - beside[8:]
         residual[0, 0, k] = load[:8] - real_applied + solved[1, 0, k]
         residual[0, 1, k] = load[8:] - imag_applied + solved[1, 1, k]
-        return carry
-
-    lax.fori_loop(0, chunks, one_residual, 0)
-
-    def drain(k, carry):
+
+    def drain(k):
         for p in range(2):
             sib_copy(p, k).wait_send()
-            for step in range(1, nrow):
-                middle_copy(p, k, step).wait_send()
-            for step in range(1, chips):
-                home_copy(p, k, step).wait_send()
-        for step in range(1, nrow):
-            load_copy(1, k, step).wait_send()
+        landed(total.at[1, k], nrow - 1, mid_send.at[1, k])
+        landed(loads.at[1, k], nrow - 1, load_send.at[1, k])
+        landed(total.at[0, k], chips - 1, arr_send.at[0, k])
+
+        @pl.when(plain)
+        def _():
+            landed(total.at[0, k], nrow - 1, mid_send.at[0, k])
+            landed(middle.at[1, k], chips - 1, arr_send.at[1, k])
 
         @pl.when(first)
         def _():
-            for step in range(1, nrow):
-                load_copy(0, k, step).wait_send()
+            landed(loads.at[0, k], nrow - 1, load_send.at[0, k])
+
+        @pl.when(crossed)
+        def _():
+            solved_copy(k).wait_send()
 
         @pl.when(jnp.logical_not(last))
         def _():
-            for other in range(nrow):
-                forward_copy(k, other).wait_send()
-
-        return carry
-
-    lax.fori_loop(0, chunks, drain, 0)
+            landed(loads.at[0, k], nrow, fwd_send.at[k])
+
+        each_edge(lambda side: edge_copy(side, k).wait_send())
+
+    def at(turn, lag, task):
+        k = turn - lag
+
+        @pl.when(jnp.logical_and(k >= 0, k < chunks))
+        def _():
+            task(k)
+
+    steps = {
+        "Ae": lambda k: multiply(0, k),
+        "Be": lambda k: combine(0, k),
+        "Re": lambda k: pass_on(0, k),
+        "Ce": finish_even,
+        "Ct": turned_sum,
+        "Rs": one_residual,
+        "Dr": drain,
+        "Ao": lambda k: multiply(1, k),
+        "Bo": lambda k: combine(1, k),
+        "Ro": lambda k: pass_on(1, k),
+        "Co": finish_odd,
+    }
+
+    def run(order):
+        def one_turn(turn, carry):
+            for name, lag in order:
+                at(turn, lag, steps[name])
+            return carry
+
+        lax.fori_loop(0, chunks + max(lag for _, lag in order), one_turn, 0)
+
+    @pl.when(plain)
+    def _():
+        run(PLAIN_ORDER)
+
+    @pl.when(later)
+    def _():
+        run(TURNED_ORDER)
+
+    @pl.when(crossed)
+    def _():
+        turned_source().wait_send()
+        each_out(lambda copy: copy.wait_send())
+
+    @pl.when(later)
+    def _():
+        each_pass(lambda half, source: pass_copy(half, source).wait_send())
 
     @pl.when(jnp.logical_not(first))
     def _():
@@ -394,23 +594,35 @@
             pltpu.VMEM((2, chunks, ROWS, 128), BF16),
             pltpu.VMEM((2, chunks, ROWS, 128), BF16),
             pltpu.VMEM(stiffness.shape, F32),
+            pltpu.VMEM((chunks, ROWS, width), BF16),
+            pltpu.VMEM((chunks, ROWS, width), BF16),
+            pltpu.VMEM((2, nrow, width // nrow, 2 * width), BF16),
+            pltpu.VMEM((chunks, ROWS, width), BF16),
+            pltpu.VMEM((chunks, ROWS, width), BF16),
             dma((2,)),
             dma((3,)),
-            dma((2, chunks, nrow - 1)),
-            dma((2, chunks)),
-            dma((2, chunks)),
-            dma((2, chunks, nrow - 1)),
-            dma((2, chunks)),
-            dma((2, chunks)),
-            dma((2, chunks)),
-            dma((2, chunks, chips - 1)),
-            dma((chunks, nrow)),
+            dma((5,)),
+            dma((2, nrow)),
+            dma((2, nrow)),
+            dma((2, nrow)),
+            dma((2, nrow)),
+            dma((chunks,)),
+            dma((chunks,)),
+            dma((2, chunks)),
+            dma((2, chunks)),
+            dma((2, chunks)),
+            dma((2, chunks)),
+            dma((2, chunks)),
+            dma((2, chunks)),
+            dma((2, chunks)),
+            dma((2, chunks)),
+            dma((chunks,)),
             dma((2,)),
-            dma((2,)),
-            dma((2,)),
+            dma((2, chunks)),
+            dma((2, chunks)),
         ],
         compiler_params=pltpu.CompilerParams(
-            collective_id=0, has_side_effects=True, vmem_limit_bytes=60 * 1024 * 1024
+            collective_id=0, has_side_effects=True, vmem_limit_bytes=52 * 1024 * 1024
         ),
         cost_estimate=pl.CostEstimate(
             flops=2 * 2 * 8 * 256 * 512 * 1024, bytes_accessed=6 * 2**20, transcendentals=0

time: 140 us -> 126 us (0.900)
  Pallas kernels: 135 us -> 121 us
    pallas_call x1, Pallas kernels: 135 us -> 121 us  [shards(): pl.pallas_call(functools.partial(sweep_kernel, groups, nrow, ncol), name=...]
    unnamed x2 -> x8, local copies, waits for them, and re-layouts: 3.54 us -> 3.94 us
where the time goes in v3:
time: 126 us; the launch traced here: 125 us
  Pallas kernels  121 us (96%)
  local copies, waits for them, and re-layouts  3.94 us (3%)
    pallas_call x1, Pallas kernels, shards(): pl.pallas_call(functools.partial(sweep_kernel, groups, nrow, ncol), name=...  121 us
    unnamed x8, local copies, waits for them, and re-layouts  3.94 us

profile of v3, /device:TPU:25, one launch (start us, length us, event | category | flops | bytes accessed | tf_op | source)
XLA Modules:
  0.0 125.4 jit_solution(11144775368551506004)
XLA Ops:
  0.6 0.0 copy-start
  0.6 1.0 copy-done
  1.7 0.0 copy-start.1
  1.7 0.8 copy-done.1
  2.4 0.0 copy-start.2
  2.4 0.7 copy-done.2
  3.1 120.8 %sweep.1 = (f32[2,2,8,8,512]{4,3,2,1,0:T(8,128)S(1)}, f32[1,2,8,8,512]{4,3,2,1,0:T(8,128)S(1)}) custom-call(f32[2,2,8,8,512]{4,3,2,1,0:T(8,128)S(1)} %copy-done, bf16[2,2,512,1024]{3,2,1,0:T(8,128)(2,1)} %inverses.1, f32[2,4096]{1,0:T(2,128)S(1)} %copy-done.1, s32[2]{0:T(128)S(1)} %copy-done.2), custom_call_target="tpu_custom_call" | custom-call | flops 4294967296 | bytes 6291456 | tf_op jit(solution)/shard_map/sweep/pallas_call | solution.py:569
  123.9 0.8 copy.8
  124.7 0.7 copy.9
Async XLA Ops:
  0.6 1.0 copy-start
  1.7 0.8 copy-start.1
  2.4 0.7 copy-start.2

commit v4 on v3

--- a/solution.py
+++ b/solution.py
@@ -13,14 +13,19 @@
 MESH = pl.DeviceIdType.MESH
 F32 = jnp.float32
 BF16 = jnp.bfloat16
+FIRST_ORDER = (
+    ("Ae", 0), ("Ce", 4), ("Rs", 12), ("Dr", 19), ("Ao", 6), ("Re", 2), ("Co", 10), ("Ro", 8), ("Be", 0), ("Bo", 6),
+)
 PLAIN_ORDER = (
-    ("Ce", 3), ("Ae", 0), ("Co", 7), ("Ao", 4), ("Be", 0), ("Re", 1), ("Bo", 4), ("Ro", 5), ("Rs", 29), ("Dr", 36),
+    ("Dr", 18), ("Ao", 6), ("Co", 9), ("Ce", 4), ("Ae", 0), ("Re", 2), ("Bo", 6), ("Be", 0), ("Rs", 12), ("Ro", 7),
 )
 TURNED_ORDER = (
-    ("Ce", 4), ("Co", 5), ("Rs", 5), ("Ao", 3), ("Ae", 0), ("Dr", 5), ("Be", 0), ("Bo", 3), ("Ct", 1),
+    ("Dr", 7), ("Co", 5), ("Ae", 0), ("Ao", 3), ("Rs", 5), ("Be", 0), ("Bo", 3), ("Ce", 3), ("Ct", 1),
 )
 PLAIN_GROUPS = 2
-SUB = 1
+WAY_STEPS = lambda n: range(n)
+WAY_HALVES = (0, 1)
+SUB = 2
 ROWS = 16
 
 
@@ -104,20 +109,9 @@
     def _():
         greet((g, r, c + 1))
 
-    in_copies[0].wait()
-    in_copies[1].wait()
-
-    @pl.when(later)
-    def _():
-        for k in range(chunks):
-            turned_out[k] = forcing[1, :, k].reshape(ROWS, width).astype(BF16)
-
-    @pl.when(jnp.logical_and(later, diagonal))
-    def _():
-        turned_forcing[...] = turned_out[...]
-
     @pl.when(first)
     def _():
+        in_copies[0].wait()
         for k in range(chunks):
             loads[0, k, r] = forcing[0, :, k].reshape(ROWS, width).astype(BF16)
 
@@ -196,11 +190,13 @@
 
     part_rows = width // nrow
 
-    def part(index):
+    sub_rows = part_rows // SUB
+
+    def part(index, sub=None):
         start = index * part_rows
-        if not isinstance(index, int):
-            start = pl.multiple_of(start, part_rows)
-        return pl.ds(start, part_rows)
+        if sub is None:
+            return pl.ds(pl.multiple_of(start, part_rows), part_rows)
+        return pl.ds(pl.multiple_of(start + sub * sub_rows, sub_rows), sub_rows)
 
     def turned_source():
         return pltpu.make_async_remote_copy(
@@ -209,12 +205,12 @@
             device_id=partner, device_id_type=MESH,
         )
 
-    def out_copy(half, q, direct):
-        rows = part(q)
+    def out_copy(half, q, sub, direct):
+        rows = part(q, sub)
         if direct:
             landing, landed_sem = weights.at[1, half, rows], part_recv.at[half, q]
         else:
-            landing, landed_sem = held.at[half, r], held_recv.at[half, r]
+            landing, landed_sem = held.at[half, r, part(0, sub)], held_recv.at[half, r, sub]
         return pltpu.make_async_remote_copy(
             src_ref=inverses.at[1, half, rows], dst_ref=landing,
             send_sem=out_send.at[half, q], recv_sem=landed_sem,
@@ -222,45 +218,49 @@
             device_id_type=MESH,
         )
 
-    def held_part(half, source):
-        here = held.at[half, source]
-        return pltpu.make_async_copy(here, here, held_recv.at[half, source])
-
-    def pass_copy(half, source):
+    def held_part(half, source, sub):
+        here = held.at[half, source, part(0, sub)]
+        return pltpu.make_async_copy(here, here, held_recv.at[half, source, sub])
+
+    def pass_copy(half, source, sub):
         index = chip if half == 0 else r
         return pltpu.make_async_remote_copy(
-            src_ref=held.at[half, source], dst_ref=weights.at[1, half, part(index)],
+            src_ref=held.at[half, source, part(0, sub)],
+            dst_ref=weights.at[1, half, part(index, sub)],
             send_sem=pass_send.at[half, source], recv_sem=part_recv.at[half, index],
             device_id=(g, r if half == 0 else chip, 2 * source + core), device_id_type=MESH,
         )
 
-    def last_part(half, q):
+    def whole_part(half, q, sem):
         here = weights.at[1, half, part(q)]
-        return pltpu.make_async_copy(here, here, part_recv.at[half, q])
-
-    def each_out(act):
-        for half, step in [(half, step) for half in range(2) for step in range(nrow)]:
+        return pltpu.make_async_copy(here, here, sem)
+
+    ways = [(half, step) for step in WAY_STEPS(nrow) for half in WAY_HALVES]
+
+    def start_out():
+        for sub in range(SUB):
+            for half, step in ways:
                 q = lax.rem((chip if half == 0 else r) + step, nrow)
 
                 @pl.when(r == q)
                 def _():
-                    act(out_copy(half, q, True))
+                    out_copy(half, q, sub, True).start()
 
                 @pl.when(r != q)
                 def _():
-                    act(out_copy(half, q, False))
+                    out_copy(half, q, sub, False).start()
 
     def each_pass(act):
-        for half, step in [(half, step) for half in range(2) for step in range(nrow)]:
-                source = lax.rem((r if half == 0 else r) + step, nrow)
-
-                @pl.when(jnp.logical_and(source != r, source != chip))
-                def _():
-                    act(half, source)
+        for half, step in ways:
+            source = lax.rem(r + step, nrow)
+
+            @pl.when(jnp.logical_and(source != r, source != chip))
+            def _():
+                act(half, source)
 
     def nf_copy():
         return pltpu.make_async_remote_copy(
-            src_ref=sources.at[0], dst_ref=next_forcing,
+            src_ref=forcing_hbm.at[0], dst_ref=next_forcing,
             send_sem=nf_sem.at[0], recv_sem=nf_sem.at[1],
             device_id=(g - 1, r, c), device_id_type=MESH,
         )
@@ -286,11 +286,15 @@
         if p == 1:
             landed(loads.at[p, k], nrow - 1, load_recv.at[p, k])
 
+            @pl.when(jnp.logical_and(jnp.logical_not(crossed), k == 0))
+            def _():
+                w_copies[1].wait()
+
             @pl.when(jnp.logical_and(crossed, k == 0))
             def _():
                 for half in range(2):
                     for q in range(nrow):
-                        last_part(half, q).wait()
+                        whole_part(half, q, part_recv.at[half, q]).wait()
         else:
             @pl.when(first)
             def _():
@@ -362,6 +366,10 @@
     def forward(k, value):
         keep(1, k, value)
 
+        @pl.when(jnp.logical_and(jnp.logical_not(last), k == 0))
+        def _():
+            nf_copy().wait_recv()
+
         @pl.when(jnp.logical_not(last))
         def _():
             source = next_forcing[:, k].reshape(ROWS, width)
@@ -419,33 +427,46 @@
     def _():
         nf_copy().start()
 
+    pl.when(crossed)(start_out)
+
+    @pl.when(later)
+    def _():
+        in_copies[1].wait()
+        for k in range(chunks):
+            turned_out[k] = forcing[1, :, k].reshape(ROWS, width).astype(BF16)
+
+        @pl.when(diagonal)
+        def _():
+            turned_forcing[...] = turned_out[...]
+
+        @pl.when(crossed)
+        def _():
+            turned_source().start()
+
+    w_copies[0].wait()
+
+    @pl.when(later)
+    def _():
+        for sub in range(SUB):
+            def pass_part(half, source):
+                held_part(half, source, sub).wait()
+                pass_copy(half, source, sub).start()
+
+            each_pass(pass_part)
+
     @pl.when(crossed)
     def _():
-        turned_source().start()
-        each_out(lambda copy: copy.start())
-
-    for copy in in_copies[2:] + w_copies[:1]:
-        copy.wait()
-
-    @pl.when(jnp.logical_not(crossed))
-    def _():
-        w_copies[1].wait()
-
-    @pl.when(later)
-    def _():
-        def pass_part(half, source):
-            held_part(half, source).wait()
-            pass_copy(half, source).start()
-
-        each_pass(pass_part)
-
-    @pl.when(crossed)
-    def _():
         turned_source().wait_recv()
 
-    @pl.when(jnp.logical_not(last))
-    def _():
-        nf_copy().wait_recv()
+    @pl.when(plain)
+    def _():
+        in_copies[1].wait()
+
+    @pl.when(jnp.logical_not(first))
+    def _():
+        in_copies[0].wait()
+
+    in_copies[2].wait()
 
     def spread(number):
         return jnp.full((8, width), number, jnp.int32).astype(F32)
@@ -538,7 +559,11 @@
 
         lax.fori_loop(0, chunks + max(lag for _, lag in order), one_turn, 0)
 
-    @pl.when(plain)
+    @pl.when(first)
+    def _():
+        run(FIRST_ORDER)
+
+    @pl.when(jnp.logical_and(plain, jnp.logical_not(first)))
     def _():
         run(PLAIN_ORDER)
 
@@ -549,11 +574,13 @@
     @pl.when(crossed)
     def _():
         turned_source().wait_send()
-        each_out(lambda copy: copy.wait_send())
+        for half in range(2):
+            for q in range(nrow):
+                whole_part(half, q, out_send.at[half, q]).wait()
 
     @pl.when(later)
     def _():
-        each_pass(lambda half, source: pass_copy(half, source).wait_send())
+        each_pass(lambda half, source: whole_part(half, 0, pass_send.at[half, source]).wait())
 
     @pl.when(jnp.logical_not(first))
     def _():
@@ -603,7 +630,7 @@
             dma((3,)),
             dma((5,)),
             dma((2, nrow)),
-            dma((2, nrow)),
+            dma((2, nrow, SUB)),
             dma((2, nrow)),
             dma((2, nrow)),
             dma((chunks,)),
@@ -622,7 +649,7 @@
             dma((2, chunks)),
         ],
         compiler_params=pltpu.CompilerParams(
-            collective_id=0, has_side_effects=True, vmem_limit_bytes=52 * 1024 * 1024
+            collective_id=0, has_side_effects=True, vmem_limit_bytes=53 * 1024 * 1024
         ),
         cost_estimate=pl.CostEstimate(
             flops=2 * 2 * 8 * 256 * 512 * 1024, bytes_accessed=6 * 2**20, transcendentals=0

time: 126 us -> 120 us (0.952)
  Pallas kernels: 121 us -> 117 us
    pallas_call x1, Pallas kernels: 121 us -> 117 us  [shards(): pl.pallas_call(functools.partial(sweep_kernel, groups, nrow, ncol), name=...]
    unnamed x8 -> x6, local copies, waits for them, and re-layouts: 3.94 us -> 2.9 us
where the time goes in v4:
time: 120 us
  Pallas kernels  117 us (98%)
  local copies, waits for them, and re-layouts  2.9 us (2%)
    pallas_call x1, Pallas kernels, shards(): pl.pallas_call(functools.partial(sweep_kernel, groups, nrow, ncol), name=...  117 us
    unnamed x6, local copies, waits for them, and re-layouts  2.9 us

profile of v4, /device:TPU:25, one launch (start us, length us, event | category | flops | bytes accessed | tf_op | source)
XLA Modules:
  0.0 120.1 jit_solution(16495979050869654253)
XLA Ops:
  0.6 0.0 copy-start
  0.6 0.7 copy-done
  1.4 0.0 copy-start.1
  1.4 0.7 copy-done.1
  2.0 116.5 %sweep.1 = (f32[2,2,8,8,512]{4,3,2,1,0:T(8,128)S(1)}, f32[1,2,8,8,512]{4,3,2,1,0:T(8,128)S(1)}) custom-call(f32[2,2,8,8,512]{4,3,2,1,0:T(8,128)} %forcing_hbm.1, bf16[2,2,512,1024]{3,2,1,0:T(8,128)(2,1)} %inverses.1, f32[2,4096]{1,0:T(2,128)S(1)} %copy-done, s32[2]{0:T(128)S(1)} %copy-done.1), custom_call_target="tpu_custom_call" | custom-call | flops 4294967296 | bytes 6291456 | tf_op jit(solution)/shard_map/sweep/pallas_call | solution.py:596
  118.6 0.8 copy.8
  119.4 0.7 copy.9
Async XLA Ops:
  0.6 0.8 copy-start
  1.4 0.7 copy-start.1

commit v5 on v4

--- a/solution.py
+++ b/solution.py
@@ -27,6 +27,10 @@
 WAY_HALVES = (0, 1)
 SUB = 2
 ROWS = 16
+
+
+def far_first(count):
+    return sorted(range(1, count), key=lambda step: -min(step, count - step))
 
 
 def sweep_kernel(
@@ -80,10 +84,10 @@
     def greet(device):
         pl.semaphore_signal(barrier, inc=1, device_id=device, device_id_type=MESH)
 
-    for step in range(1, nrow):
+    for step in far_first(nrow):
         greet(column(lax.rem(r + step, nrow)))
     greet((g, r, sibling))
-    for step in range(1, chips):
+    for step in far_first(chips):
         greet(along(lax.rem(chip + step, chips)))
     for other in range(nrow):
         @pl.when(jnp.logical_not(last))
@@ -96,9 +100,9 @@
 
     @pl.when(crossed)
     def _():
-        for step in range(1, chips):
+        for step in far_first(chips):
             greet((g, chip, 2 * lax.rem(chip + step, chips) + core))
-        for step in range(1, nrow):
+        for step in far_first(nrow):
             greet((g, lax.rem(r + step, nrow), 2 * r + core))
 
     @pl.when(jnp.logical_not(left_end))
@@ -328,7 +332,7 @@
 
         def to_rows():
             middle[p, k, r] = total[p, k, r]
-            for step in range(1, nrow):
+            for step in far_first(nrow):
                 middle_copy(p, k, step).start()
 
         if p == 1:
@@ -339,7 +343,7 @@
             @pl.when(later)
             def _():
                 arrive[p, k, chip] = total[p, k, chip]
-                for step in range(1, chips):
+                for step in far_first(chips):
                     row_copy(p, k, step).start()
 
     def row_sum(p, k):
@@ -351,7 +355,7 @@
 
     def pass_on(p, k):
         middle_landed(p, k)
-        for step in range(1, chips):
+        for step in far_first(chips):
             home_copy(p, k, step).start()
         arrive[p, k, chip] = middle[p, k, chip]
 
@@ -374,13 +378,13 @@
         def _():
             source = next_forcing[:, k].reshape(ROWS, width)
             onward[k] = (value + source).astype(BF16)
-            for other in range(nrow):
-                forward_copy(k, other).start()
+            for step in far_first(nrow) + [0]:
+                forward_copy(k, lax.rem(r + step, nrow)).start()
 
     def turned_sum(k):
         own = row_sum(0, k)
         loads[1, k, chip] = (own + turned_forcing[k].astype(F32)).astype(BF16)
-        for step in range(1, chips):
+        for step in far_first(chips):
             row_load_copy(k, step).start()
 
         @pl.when(diagonal)
@@ -399,7 +403,7 @@
             keep(0, k, value)
             source = forcing[1, :, k].reshape(ROWS, width)
             loads[1, k, r] = (value + source).astype(BF16)
-            for step in range(1, nrow):
+            for step in far_first(nrow):
                 load_copy(1, k, step).start()
 
         @pl.when(crossed)
@@ -420,7 +424,7 @@
     @pl.when(first)
     def _():
         for k in range(chunks):
-            for step in range(1, nrow):
+            for step in far_first(nrow):
                 load_copy(0, k, step).start()
 
     @pl.when(jnp.logical_not(first))

time: 120 us -> 116 us (0.967)
  Pallas kernels: 117 us -> 112 us
    pallas_call x1, Pallas kernels: 117 us -> 112 us  [shards(): pl.pallas_call(functools.partial(sweep_kernel, groups, nrow, ncol), name=...]
where the time goes in v5:
time: 116 us
  Pallas kernels  112 us (97%)
  local copies, waits for them, and re-layouts  2.9 us (2%)
    pallas_call x1, Pallas kernels, shards(): pl.pallas_call(functools.partial(sweep_kernel, groups, nrow, ncol), name=...  112 us
    unnamed x6, local copies, waits for them, and re-layouts  2.9 us

profile of v5, /device:TPU:25, one launch (start us, length us, event | category | flops | bytes accessed | tf_op | source)
XLA Modules:
  0.0 115.6 jit_solution(10228080701530333480)
XLA Ops:
  0.6 0.0 copy-start
  0.6 0.7 copy-done
  1.4 0.0 copy-start.1
  1.4 0.7 copy-done.1
  2.0 112.0 %sweep.1 = (f32[2,2,8,8,512]{4,3,2,1,0:T(8,128)S(1)}, f32[1,2,8,8,512]{4,3,2,1,0:T(8,128)S(1)}) custom-call(f32[2,2,8,8,512]{4,3,2,1,0:T(8,128)} %forcing_hbm.1, bf16[2,2,512,1024]{3,2,1,0:T(8,128)(2,1)} %inverses.1, f32[2,4096]{1,0:T(2,128)S(1)} %copy-done, s32[2]{0:T(128)S(1)} %copy-done.1), custom_call_target="tpu_custom_call" | custom-call | flops 4294967296 | bytes 6291456 | tf_op jit(solution)/shard_map/sweep/pallas_call | solution.py:600
  114.1 0.8 copy.8
  114.9 0.7 copy.9
Async XLA Ops:
  0.6 0.8 copy-start
  1.4 0.7 copy-start.1

commit v6 on v5

--- a/solution.py
+++ b/solution.py
@@ -368,8 +368,6 @@
             each_edge(lambda side: edge_copy(side, k).start())
 
     def forward(k, value):
-        keep(1, k, value)
-
         @pl.when(jnp.logical_and(jnp.logical_not(last), k == 0))
         def _():
             nf_copy().wait_recv()
@@ -380,6 +378,8 @@
             onward[k] = (value + source).astype(BF16)
             for step in far_first(nrow) + [0]:
                 forward_copy(k, lax.rem(r + step, nrow)).start()
+
+        keep(1, k, value)
 
     def turned_sum(k):
         own = row_sum(0, k)
@@ -400,11 +400,11 @@
         @pl.when(plain)
         def _():
             value = row_sum(0, k)
-            keep(0, k, value)
             source = forcing[1, :, k].reshape(ROWS, width)
             loads[1, k, r] = (value + source).astype(BF16)
             for step in far_first(nrow):
                 load_copy(1, k, step).start()
+            keep(0, k, value)
 
         @pl.when(crossed)
         def _():

time: 116 us -> 116 us (level)
  no operation moved by 1% of the time
where the time goes in v6:
time: 116 us
  Pallas kernels  112 us (97%)
  local copies, waits for them, and re-layouts  2.9 us (2%)
    pallas_call x1, Pallas kernels, shards(): pl.pallas_call(functools.partial(sweep_kernel, groups, nrow, ncol), name=...  112 us
    unnamed x6, local copies, waits for them, and re-layouts  2.9 us

profile of v6, /device:TPU:25, one launch (start us, length us, event | category | flops | bytes accessed | tf_op | source)
XLA Modules:
  0.0 115.6 jit_solution(1983455334566696283)
XLA Ops:
  0.6 0.0 copy-start
  0.6 0.7 copy-done
  1.4 0.0 copy-start.1
  1.4 0.7 copy-done.1
  2.0 112.0 %sweep.1 = (f32[2,2,8,8,512]{4,3,2,1,0:T(8,128)S(1)}, f32[1,2,8,8,512]{4,3,2,1,0:T(8,128)S(1)}) custom-call(f32[2,2,8,8,512]{4,3,2,1,0:T(8,128)} %forcing_hbm.1, bf16[2,2,512,1024]{3,2,1,0:T(8,128)(2,1)} %inverses.1, f32[2,4096]{1,0:T(2,128)S(1)} %copy-done, s32[2]{0:T(128)S(1)} %copy-done.1), custom_call_target="tpu_custom_call" | custom-call | flops 4294967296 | bytes 6291456 | tf_op jit(solution)/shard_map/sweep/pallas_call | solution.py:600
  114.1 0.8 copy.8
  114.9 0.7 copy.9
Async XLA Ops:
  0.6 0.8 copy-start
  1.4 0.7 copy-start.1
